TPU v7x, 256 devices: a whole 4x4x8 slice. The times are simulated.
256 devices in a mesh: dp: 32 (over x, y, core), tensor: 8 (over z).
Axes of the slice: x: 4, y: 4, z: 8, core: 2. Of those that a mesh axis runs over, the one named last changes fastest.
Arguments:
- hidden: bfloat16 [32768, 28672], P('dp', 'tensor'), may hold values from -6 to 6
- out_grad: bfloat16 [32768, 8192], P('dp', 'tensor'), may hold values from -6 to 6
- lengths: int32 [64], P('dp'), may hold values from 128 to 512, as said below
- hid_kind: int32 [224], P('tensor'), may hold values from 0 to 7
- hid_sign: int32 [224], P('tensor'), may hold values from 0 to 1
- hid_table: bfloat16 [8, 128, 32], replicated, may hold values from -0.03125 to 0.03125
- out_kind: int32 [64], P('tensor'), may hold values from 0 to 7
- out_sign: int32 [64], P('tensor'), may hold values from 0 to 1
- out_table: bfloat16 [8, 128, 32], replicated, may hold values from -0.0625 to 0.0625
- ridge: float32 [1], replicated, may hold values from 256 to 2048
Outputs:
- whitened: float32 [64, 1024], P('dp')
Inputs may be any that keep to these rules, and one draw needn't show every extreme that they name: `lengths`: some sequence has exactly 512 tokens.
All inputs are finite; a program needn't handle non-finite values.
Results may differ from a plain program's by a relative error of at most 0.0003.
Values sent between devices are 32-bit elements; how exact they have to be, the bound alone decides.
No kernel may reach another device: no remote copies, remote signals or barrier semaphores. Data moves between devices by JAX's collectives and lax.ppermute only.
A program may use at most 128 MiB of HBM per device.

v0:
```python
import jax
import jax.numpy as jnp
from jax import lax
from jax.sharding import PartitionSpec as P


def sketch_matrix(kinds, signs, table):
    picks = (kinds[:, None] == jnp.arange(table.shape[0], dtype=jnp.int32)[None, :]).astype(
        jnp.float32
    )
    picks = picks * (2 * signs - 1).astype(jnp.float32)[:, None]
    blocks = jnp.einsum(
        "jk,kcm->jcm", picks, table.astype(jnp.float32), precision=lax.Precision.HIGHEST
    )
    return blocks.reshape(-1, table.shape[2]).astype(jnp.bfloat16)


def seq_features(left, right, lengths, seq_len):
    count = left.shape[0]
    slots = lengths.shape[0]
    places = jnp.arange(count, dtype=jnp.int32)
    owner = places // seq_len
    offset = places % seq_len
    member = (owner[:, None] == jnp.arange(slots, dtype=jnp.int32)[None, :]) & (
        offset[:, None] < lengths[None, :]
    )
    weights = member.astype(jnp.float32) * lax.rsqrt(lengths.astype(jnp.float32))[None, :]
    outer = jnp.einsum("ts,tm,tn->smn", weights, left, right, precision=lax.Precision.HIGHEST)
    return outer.reshape(slots, -1)


def per_device(
    hidden, out_grad, lengths, hid_kind, hid_sign, hid_table, out_kind, out_sign, out_table, ridge
):
    s_in = sketch_matrix(hid_kind, hid_sign, hid_table)
    s_out = sketch_matrix(out_kind, out_sign, out_table)
    left_part = jnp.dot(hidden, s_in, preferred_element_type=jnp.float32)
    right_part = jnp.dot(out_grad, s_out, preferred_element_type=jnp.float32)
    seq_len = hidden.shape[0] // lengths.shape[0]
    left, right = lax.psum((left_part, right_part), "tensor")
    feats = seq_features(left, right, lengths, seq_len)
    width = feats.shape[1]
    local_gram = jnp.dot(feats.T, feats, precision=lax.Precision.HIGHEST)
    gram = lax.psum(local_gram, "dp")
    gram = gram + ridge[0] * jnp.eye(width, dtype=jnp.float32)
    lower = jnp.linalg.cholesky(gram)
    solved = jax.scipy.linalg.solve_triangular(lower, feats.T, lower=True)
    return solved.T * jnp.sqrt(jnp.float32(width))


def solution(mesh):
    return jax.shard_map(
        per_device,
        mesh=mesh,
        in_specs=(
            P("dp", "tensor"),
            P("dp", "tensor"),
            P("dp"),
            P("tensor"),
            P("tensor"),
            P(),
            P("tensor"),
            P("tensor"),
            P(),
            P(),
        ),
        out_specs=P("dp", None),
        check_vma=False,
    )
```

profile of v0, /device:TPU:1, one launch (start us, length us, event | category | flops | bytes accessed | tf_op | source)
XLA Modules:
  0.0 575.9 jit_solution(9620547310219930471)
XLA Ops:
  11.8 6.0 %convolution_bitcast_fusion.1 = f32[1024,32]{0,1:T(8,128)} fusion(bf16[1024,3584]{1,0:T(8,128)(2,1)} %param.10, bf16[4,8,28,128]{3,2,1,0:T(8,128)(2,1)S(1)} %bitcast.136), kind=kOutput, calls=%fused_computation.21 | convolution fusion | flops 234881024 | bytes 7700480 | tf_op jit(solution)/shard_map/dot_general | solution.py:37
  18.0 71.9 %all-reduce.7.cloned.1.call-done = (f32[1024,32]{0,1:T(8,128)}, f32[1024,32]{0,1:T(8,128)}) async-done(((f32[1024,32]{0,1:T(8,128)}, f32[1024,32]{0,1:T(8,128)}), (f32[1024,32]{0,1:T(8,128)}, f32[1024,32]{0,1:T(8,128)})) %all-reduce.7.cloned.1.call-update) | async-done | bytes 262160 | tf_op jit(solution)/shard_map/psum | solution.py:40
  91.3 5.0 fusion.91
  97.6 123.6 %all-reduce.5.cloned.1.call-done = f32[1024,1024]{0,1:T(8,128)} async-done(((f32[1024,1024]{0,1:T(8,128)}), f32[1024,1024]{0,1:T(8,128)}) %all-reduce.5.cloned.1.call-update) | async-done | bytes 4194320 | tf_op jit(solution)/shard_map/psum | solution.py:44
  221.2 4.8 select_add_fusion
  226.0 5.6 copy.34
  231.6 4.5 fusion
  238.0 11.7 %cholesky.222 = f32[128,128]{1,0:T(8,128)S(1)} custom-call(f32[128,128]{1,0:T(8,128)S(1)} %cholesky.577), custom_call_target="Cholesky" | custom-call | tf_op jit(solution)/shard_map/jit(cholesky)/cholesky | solution.py:46
  249.9 9.8 %custom-call.63 = f32[1,128,128]{1,2,0:T(8,128)S(1)} custom-call(f32[1,128,128]{2,1,0:T(8,128)S(1)} %get-tuple-element.46), custom_call_target="InvertDiagBlocksLowerTriangular" | custom-call | tf_op jit(solution)/shard_map/jit(cholesky)/cholesky | solution.py:46
  263.0 11.7 %cholesky.243 = f32[128,128]{1,0:T(8,128)S(1)} custom-call(f32[128,128]{1,0:T(8,128)S(1)} %cholesky.581), custom_call_target="Cholesky" | custom-call | tf_op jit(solution)/shard_map/jit(cholesky)/cholesky | solution.py:46
  275.4 9.8 %custom-call.64 = f32[1,128,128]{1,2,0:T(8,128)S(1)} custom-call(f32[1,128,128]{2,1,0:T(8,128)S(1)} %get-tuple-element.44), custom_call_target="InvertDiagBlocksLowerTriangular" | custom-call | tf_op jit(solution)/shard_map/jit(cholesky)/cholesky | solution.py:46
  288.3 2.4 convolution_subtract_fusion.1
  290.7 11.7 %cholesky.466 = f32[128,128]{1,0:T(8,128)S(1)} custom-call(f32[128,128]{1,0:T(8,128)S(1)} %cholesky.586), custom_call_target="Cholesky" | custom-call | tf_op jit(solution)/shard_map/jit(cholesky)/cholesky | solution.py:46
  303.2 9.8 %custom-call.65 = f32[1,128,128]{1,2,0:T(8,128)S(1)} custom-call(f32[1,128,128]{2,1,0:T(8,128)S(1)} %get-tuple-element.42), custom_call_target="InvertDiagBlocksLowerTriangular" | custom-call | tf_op jit(solution)/shard_map/jit(cholesky)/cholesky | solution.py:46
  314.3 3.3 convolution_subtract_fusion.2
  317.6 11.7 %cholesky.485 = f32[128,128]{1,0:T(8,128)S(1)} custom-call(f32[128,128]{1,0:T(8,128)S(1)} %cholesky.591), custom_call_target="Cholesky" | custom-call | tf_op jit(solution)/shard_map/jit(cholesky)/cholesky | solution.py:46
  330.1 9.8 %custom-call.66 = f32[1,128,128]{1,2,0:T(8,128)S(1)} custom-call(f32[1,128,128]{2,1,0:T(8,128)S(1)} %get-tuple-element.40), custom_call_target="InvertDiagBlocksLowerTriangular" | custom-call | tf_op jit(solution)/shard_map/jit(cholesky)/cholesky | solution.py:46
  341.0 3.1 convolution_subtract_fusion.3
  344.2 11.9 %cholesky.504 = f32[128,128]{1,0:T(8,128)S(1)} custom-call(f32[128,128]{1,0:T(8,128)S(1)} %cholesky.596), custom_call_target="Cholesky" | custom-call | tf_op jit(solution)/shard_map/jit(cholesky)/cholesky | solution.py:46
  356.9 9.8 %custom-call.67 = f32[1,128,128]{1,2,0:T(8,128)S(1)} custom-call(f32[1,128,128]{2,1,0:T(8,128)S(1)} %get-tuple-element.38), custom_call_target="InvertDiagBlocksLowerTriangular" | custom-call | tf_op jit(solution)/shard_map/jit(cholesky)/cholesky | solution.py:46
  367.8 3.1 convolution_subtract_fusion.4
  370.9 11.7 %cholesky.524 = f32[128,128]{1,0:T(8,128)S(1)} custom-call(f32[128,128]{1,0:T(8,128)S(1)} %cholesky.601), custom_call_target="Cholesky" | custom-call | tf_op jit(solution)/shard_map/jit(cholesky)/cholesky | solution.py:46
  383.4 9.8 %custom-call.68 = f32[1,128,128]{1,2,0:T(8,128)S(1)} custom-call(f32[1,128,128]{2,1,0:T(8,128)S(1)} %get-tuple-element.36), custom_call_target="InvertDiagBlocksLowerTriangular" | custom-call | tf_op jit(solution)/shard_map/jit(cholesky)/cholesky | solution.py:46
  394.2 3.1 convolution_subtract_fusion.5
  397.3 11.7 %cholesky.544 = f32[128,128]{1,0:T(8,128)S(1)} custom-call(f32[128,128]{1,0:T(8,128)S(1)} %cholesky.606), custom_call_target="Cholesky" | custom-call | tf_op jit(solution)/shard_map/jit(cholesky)/cholesky | solution.py:46
  409.8 9.8 %custom-call.69 = f32[1,128,128]{1,2,0:T(8,128)S(1)} custom-call(f32[1,128,128]{2,1,0:T(8,128)S(1)} %get-tuple-element.34), custom_call_target="InvertDiagBlocksLowerTriangular" | custom-call | tf_op jit(solution)/shard_map/jit(cholesky)/cholesky | solution.py:46
  422.6 11.7 %cholesky.562 = f32[128,128]{1,0:T(8,128)S(1)} custom-call(f32[128,128]{1,0:T(8,128)S(1)} %convolution_subtract_fusion.6), custom_call_target="Cholesky" | custom-call | tf_op jit(solution)/shard_map/jit(cholesky)/cholesky | solution.py:46
  445.4 4.8 select_select_fusion
  450.3 28.5 %while.1 = (s32[]{:T(128)}, f32[1024,1024]{0,1:T(8,128)}, s32[8,2]{0,1:T(2,128)S(1)}, f32[8,128,128]{2,1,0:T(8,128)}, s32[]{:T(128)}) while((s32[]{:T(128)}, f32[1024,1024]{0,1:T(8,128)}, s32[8,2]{0,1:T(2,128)S(1)}, f32[8,128,128]{2,1,0:T(8,128)}, s32[]{:T(128)}) %tuple.51), condition=%wide.while_cond, body=%wide.while_body.sunk | while | flops 2 | bytes 393329 | solution.py:47
  450.9 2.2 dynamic-slice.7
  458.0 2.2 dynamic-slice.7
  478.8 79.5 %custom-call.70 = f32[8,128,128]{1,2,0:T(8,128)S(1)} custom-call(f32[8,128,128]{2,1,0:T(8,128)} %get-tuple-element.12), custom_call_target="InvertDiagBlocksLowerTriangular" | custom-call | tf_op jit(solution)/shard_map/jit(_solve_triangular)/triangular_solve | solution.py:47
  (131 shorter events, 68.3 us)
Async XLA Ops:
  6.5 2.6 copy-start
  6.5 83.3 %all-reduce.7.cloned.1.call-start = ((), (), s32[]{:S(2)}) async-start(), calls=%async_computation.1 | async-start | bytes 524288 | tf_op jit(solution)/shard_map/psum | solution.py:40
  10.5 7.3 %copy-start.3 = (s32[2]{0:T(128)S(1)}, s32[2]{0:T(128)}, u32[]{:S(2)}) copy-start(s32[2]{0:T(128)} %param.12) | copy-start | bytes 28
  17.8 203.4 %all-reduce.5.cloned.1.call-start = ((), (), s32[]{:S(2)}) async-start(), calls=%async_computation | async-start | bytes 8388608 | tf_op jit(solution)/shard_map/psum | solution.py:44
  236.1 1.9 copy-start.2
  286.3 2.0 copy-start.1
  445.4 4.8 copy-start.4
Sparse Core Ops, SparseCore 0:
  17.9 71.9 all-reduce.6
  96.5 124.6 all-reduce.4
where the time goes:
time: 581 us; the launch traced here: 576 us
  other arithmetic  265 us (46%)
  waiting for transfers between devices  196 us (34%)
  matrix products  52.1 us (9%)
  local copies, waits for them, and re-layouts  43.9 us (8%)
  between operations  19.6 us (3%)
    another operation x31, other arithmetic, per_device(): lower = jnp.linalg.cholesky(gram)  168 us
    psum x1, waiting for transfers between devices, per_device(): gram = lax.psum(local_gram, 'dp')  124 us
    another operation x3, other arithmetic, per_device(): solved = jax.scipy.linalg.solve_triangular(lower, feats.T, lower=True)  84.9 us
    psum x1, waiting for transfers between devices, per_device(): left, right = lax.psum((left_part, right_part), 'tensor')  71.9 us
    another operation x40, local copies, waits for them, and re-layouts  28.4 us
    another operation x14, matrix products, per_device(): lower = jnp.linalg.cholesky(gram)  26.1 us
  transfers between devices with their start and end apart: 2, of which 2 were waited for; matrix products, arithmetic and copies ran while one was open for 0% of the time, Pallas kernels for 0%

commit v1 on v0

v1 whole, which is shorter than its diff:
```python
import functools

import jax
import jax.numpy as jnp
from jax import lax
from jax.experimental import pallas as pl
from jax.experimental.pallas import tpu as pltpu
from jax.sharding import PartitionSpec as P

F32 = jnp.float32
BF16 = jnp.bfloat16
LANES = 128
SUB = 8
VMEM = pl.BlockSpec(memory_space=pltpu.VMEM)
SMEM = pl.BlockSpec(memory_space=pltpu.SMEM)
HBM = pl.BlockSpec(memory_space=pl.ANY)


def iota(shape, dim):
    return lax.broadcasted_iota(jnp.int32, shape, dim)


def sketch_kernel(
    which, hid_kind, hid_sign, out_kind, out_sign, hid_table, out_table, hidden, out_grad, x,
    hid_buf, out_buf, hid_pad, out_pad, s_in, s_out, hid_sems, out_sems,
):
    chunks, rows, _ = hid_buf.shape
    first = which[0] * (chunks * rows)
    copies = []
    for c in range(chunks):
        here = pl.ds(pl.multiple_of(first + c * rows, rows), rows)
        copies.append(
            (
                pltpu.make_async_copy(hidden.at[here], hid_buf.at[c], hid_sems.at[c]),
                pltpu.make_async_copy(out_grad.at[here], out_buf.at[c], out_sems.at[c]),
            )
        )
    for pair in copies:
        for copy in pair:
            copy.start()
    kinds, depth, width = hid_table.shape
    zero = jnp.zeros((depth, width), BF16)
    for k in range(kinds):
        hid_pad[k] = jnp.concatenate([hid_table[k], zero, zero, zero], axis=1)
        out_pad[k] = jnp.concatenate([zero, out_table[k], zero, zero], axis=1)

    def fill(kind, sign, pad, s):
        for j in range(kind.shape[0]):
            block = pad[kind[j]]
            s[pl.ds(j * depth, depth), :] = jnp.where(sign[j] > 0, block, -block)

    fill(hid_kind, hid_sign, hid_pad, s_in)
    fill(out_kind, out_sign, out_pad, s_out)
    for c in range(chunks):
        for copy in copies[c]:
            copy.wait()
        part = jnp.dot(hid_buf[c], s_in[...], preferred_element_type=F32)
        part += jnp.dot(out_buf[c], s_out[...], preferred_element_type=F32)
        if c < chunks // 2:
            x[pl.ds(c * rows, rows), :] = part
        else:
            x[pl.ds((c - chunks // 2) * rows, rows), :] += pltpu.roll(part, 2 * width, 1)


def sketch(which, hidden, out_grad, hid_kind, hid_sign, hid_table, out_kind, out_sign, out_table, length):
    chunks = 4
    rows = length // chunks
    deep, wide = hidden.shape[1], out_grad.shape[1]
    return pl.pallas_call(
        sketch_kernel,
        out_shape=jax.ShapeDtypeStruct((length // 2, LANES), F32),
        in_specs=[SMEM] * 5 + [VMEM] * 2 + [HBM] * 2,
        out_specs=VMEM,
        scratch_shapes=[
            pltpu.VMEM((chunks, rows, deep), BF16),
            pltpu.VMEM((chunks, rows, wide), BF16),
            pltpu.VMEM(hid_table.shape[:2] + (LANES,), BF16),
            pltpu.VMEM(out_table.shape[:2] + (LANES,), BF16),
            pltpu.VMEM((deep, LANES), BF16),
            pltpu.VMEM((wide, LANES), BF16),
            pltpu.SemaphoreType.DMA((chunks,)),
            pltpu.SemaphoreType.DMA((chunks,)),
        ],
        compiler_params=pltpu.CompilerParams(vmem_limit_bytes=24 * 2**20),
        name="sketch",
    )(which, hid_kind, hid_sign, out_kind, out_sign, hid_table, out_table, hidden, out_grad)


def outer_kernel(which, lengths, x_ref, other, feats):
    x = x_ref[...] + other[...]
    half = x.shape[0]
    count = lengths[which[0]]
    lane = iota(x.shape, 1)
    place = iota(x.shape, 0) + jnp.where(lane >= LANES // 2, half, 0)
    live = jnp.where(place < count, x, 0.0)
    z = lax.dot_general(
        live, x, (((0,), (0,)), ((), ())), precision=lax.Precision.HIGHEST, preferred_element_type=F32
    )
    row, column = iota((LANES, LANES), 0), iota((LANES, LANES), 1)
    spread = (row == column // 4).astype(F32)
    spread_later = (row - LANES // 2 == column // 4).astype(F32)
    quarter = LANES // 4
    y = jnp.dot(
        z[quarter : 2 * quarter], spread, precision=lax.Precision.HIGHEST, preferred_element_type=F32
    ) + jnp.dot(
        z[3 * quarter :], spread_later, precision=lax.Precision.HIGHEST, preferred_element_type=F32
    )
    own = iota((SUB, LANES), 1) % 4
    total = jnp.zeros((SUB, LANES), F32)
    for q in range(4):
        total += jnp.where(own == q, y[q * SUB : (q + 1) * SUB], 0.0)
    feats[...] = total * lax.rsqrt(jnp.full((SUB, LANES), count, jnp.int32).astype(F32))


def outer(which, lengths, x, other):
    return pl.pallas_call(
        outer_kernel,
        out_shape=jax.ShapeDtypeStruct((SUB, LANES), F32),
        in_specs=[SMEM, SMEM, VMEM, VMEM],
        out_specs=VMEM,
        name="outer",
    )(which, lengths, x, other)


def split(x, parts):
    out = []
    for _ in range(parts):
        piece = x.astype(BF16)
        out.append(piece)
        x = x - piece.astype(F32)
    return out


def whiten_kernel(place, ridge, gathered, out, aug, across, prods):
    seqs = 2 * gathered.shape[0]
    groups = seqs // SUB
    last = gathered.shape[0] - 1
    own = place[0]
    r = ridge[0]
    for g in range(gathered.shape[0]):
        src = gathered[g]
        aug[2 * g, seqs : seqs + SUB, :] = src[:SUB]
        aug[2 * g + 1, seqs : seqs + SUB, :] = src[SUB:]
    mine, tail = gathered[own], gathered[last]
    for h in range(2):
        aug[2 * own + h, seqs : seqs + SUB, :] = tail[h * SUB : (h + 1) * SUB]
        aug[2 * last + h, seqs : seqs + SUB, :] = mine[h * SUB : (h + 1) * SUB]
    for f in range(SUB):
        for i in range(seqs):
            across[f, i : i + 1, :] = aug[i, seqs + f : seqs + f + 1, :]
    for f in range(SUB):
        aug[seqs + f, seqs : seqs + SUB, :] = jnp.zeros((SUB, LANES), F32)

    def products(i8, _):
        def inner(j8, _):
            for ii in range(SUB):
                i = i8 * SUB + ii
                acc = jnp.zeros((SUB, LANES), F32)
                for f in range(SUB):
                    acc += aug[i, pl.ds(seqs + f, 1), :] * across[f, pl.ds(pl.multiple_of(j8 * SUB, SUB), SUB), :]
                prods[i, pl.ds(pl.multiple_of(j8 * SUB, SUB), SUB), :] = acc
            return 0

        return lax.fori_loop(i8, groups, inner, 0)

    lax.fori_loop(0, groups, products, 0)
    before = (iota((LANES, LANES), 0) < iota((LANES, LANES), 1)).astype(BF16)
    for i8 in range(groups):
        wide = seqs - i8 * SUB
        block = prods[i8 * SUB : (i8 + 1) * SUB, i8 * SUB : seqs, :].reshape(SUB * wide, LANES)
        total = sum(jnp.dot(piece, before, preferred_element_type=F32) for piece in split(block, 3))
        aug[i8 * SUB : (i8 + 1) * SUB, i8 * SUB : seqs, :] = total.reshape(SUB, wide, LANES)
    sub = iota((SUB, LANES), 0)
    for i8 in range(groups):
        for ii in range(SUB):
            i = i8 * SUB + ii
            aug[i, i8 * SUB : (i8 + 1) * SUB, :] += jnp.where(sub == ii, r, 0.0)

    for p in range(groups):
        base = p * SUB
        diag = [aug[base + k, base : base + SUB, :] for k in range(SUB)]
        inv = []
        for k in range(SUB):
            inv.append(lax.rsqrt(diag[k][k : k + 1]))
            diag[k] = diag[k] * inv[k]
            for i in range(k + 1, SUB):
                diag[i] = diag[i] - diag[k][i : i + 1] * diag[k]
        for k in range(SUB):
            aug[base + k, base : base + SUB, :] = diag[k]
        for j8 in range(p + 1, groups + 1):
            rows = [aug[base + k, j8 * SUB : (j8 + 1) * SUB, :] for k in range(SUB)]
            for k in range(SUB):
                rows[k] = rows[k] * inv[k]
                for i in range(k + 1, SUB):
                    rows[i] = rows[i] - diag[k][i : i + 1] * rows[k]
            for k in range(SUB):
                aug[base + k, j8 * SUB : (j8 + 1) * SUB, :] = rows[k]

        def trail(i8, _):
            def inner(j8, _):
                cols = pl.ds(pl.multiple_of(j8 * SUB, SUB), SUB)
                rows = [aug[base + k, cols, :] for k in range(SUB)]
                for ii in range(SUB):
                    acc = aug[i8 * SUB + ii, cols, :]
                    for k in range(SUB):
                        acc -= aug[base + k, pl.ds(i8 * SUB + ii, 1), :] * rows[k]
                    aug[i8 * SUB + ii, cols, :] = acc
                return 0

            return lax.fori_loop(i8, groups + 1, inner, 0)

        lax.fori_loop(p + 1, groups + 1, trail, 0)

    end = seqs - 1
    sol_end = aug[end, seqs : seqs + SUB, :] / aug[end, end : end + 1, :]
    sol = (aug[end - 1, seqs : seqs + SUB, :] - aug[end - 1, end : end + 1, :] * sol_end) / aug[
        end - 1, end - 1 : end, :
    ]
    x = [sol * r, sol_end * r]
    schur = [jnp.where(sub == f, r, 0.0) - r * aug[seqs + f, seqs : seqs + SUB, :] for f in range(SUB)]
    w = [jnp.zeros((SUB, LANES), F32) for _ in range(2)]
    for f in range(SUB):
        scale = lax.rsqrt(schur[f][f : f + 1])
        line = schur[f] * scale
        for i in range(f + 1, SUB):
            schur[i] = schur[i] - line[i : i + 1] * line
        for h in range(2):
            value = x[h][f : f + 1] * scale
            w[h] = jnp.where(sub == f, value, w[h])
            x[h] = x[h] - line * value
    size = SUB * LANES
    w = jnp.concatenate(w, axis=0) * jnp.sqrt(jnp.full((2 * SUB, LANES), size, F32))
    spread = (iota((LANES, size), 0) == iota((LANES, size), 1) // SUB).astype(BF16)
    wide = sum(jnp.dot(piece, spread, preferred_element_type=F32) for piece in split(w, 3))
    wide = jnp.where(iota((2 * SUB, size), 1) % SUB == iota((2 * SUB, size), 0) % SUB, wide, 0.0)
    lines = [jnp.sum(wide[h * SUB : (h + 1) * SUB], axis=0, keepdims=True) for h in range(2)]
    swap = place[1] > 0
    out[0:1, :] = jnp.where(swap, lines[1], lines[0])
    out[1:2, :] = jnp.where(swap, lines[0], lines[1])


def whiten(place, ridge, gathered):
    seqs = 2 * gathered.shape[0]
    return pl.pallas_call(
        whiten_kernel,
        out_shape=jax.ShapeDtypeStruct((2, SUB * LANES), F32),
        in_specs=[SMEM, SMEM, VMEM],
        out_specs=VMEM,
        scratch_shapes=[
            pltpu.VMEM((seqs + SUB, seqs + SUB, LANES), F32),
            pltpu.VMEM((SUB, seqs, LANES), F32),
            pltpu.VMEM((seqs, seqs, LANES), F32),
        ],
        compiler_params=pltpu.CompilerParams(vmem_limit_bytes=24 * 2**20),
        name="whiten",
    )(place, ridge, gathered)


def per_device(
    dp, tensor,
    hidden, out_grad, lengths, hid_kind, hid_sign, hid_table, out_kind, out_sign, out_table, ridge
):
    z = lax.axis_index("tensor")
    odd = (z % 2).astype(jnp.int32)
    length = hidden.shape[0] // lengths.shape[0]

    def of(which):
        return sketch(
            which.reshape(1), hidden, out_grad, hid_kind, hid_sign, hid_table, out_kind, out_sign, out_table, length
        )

    def swap(x, bit):
        return lax.ppermute(x, "tensor", [(i, i ^ bit) for i in range(tensor)])

    away = swap(of(1 - odd), 1)
    x = of(odd) + away
    x = x + swap(x, 2)
    feats = outer(odd.reshape(1), lengths, x, swap(x, 4))
    both = jnp.concatenate([feats, swap(feats, 1)], axis=0)
    gathered = lax.all_to_all(jnp.broadcast_to(both[None], (dp,) + both.shape), "dp", 0, 0)
    place = jnp.stack([lax.axis_index("dp").astype(jnp.int32), odd])
    return whiten(place, ridge, gathered)


def solution(mesh):
    return jax.shard_map(
        functools.partial(per_device, mesh.shape["dp"], mesh.shape["tensor"]),
        mesh=mesh,
        in_specs=(
            P("dp", "tensor"),
            P("dp", "tensor"),
            P("dp"),
            P("tensor"),
            P("tensor"),
            P(),
            P("tensor"),
            P("tensor"),
            P(),
            P(),
        ),
        out_specs=P("dp", None),
        check_vma=False,
    )
```

time: 581 us -> 81.4 us (0.14)
  other arithmetic: 265 us -> 0.8 us
  waiting for transfers between devices: 196 us -> 21.2 us
  matrix products: 52.1 us -> 0 us
  local copies, waits for them, and re-layouts: 43.9 us -> 10.7 us
  Pallas kernels: 0 us -> 24.5 us
  starting transfers between devices: 0.04 us -> 23 us
  between operations: 19.6 us -> 0.74 us
    another operation x34 -> x1, other arithmetic: 253 us -> 0.08 us  [per_device(): place = jnp.stack([lax.axis_index('dp').astype(jnp.int32), odd])]
    psum x2 -> x0, waiting for transfers between devices: 196 us -> none  [the longest x1 124 us: per_device(): gram = lax.psum(local_gram, 'dp')]
    another operation x29 -> x0, matrix products: 36 us -> none  [the longest x14 26.1 us: per_device(): lower = jnp.linalg.cholesky(gram)]
    another operation x66 -> x0, local copies, waits for them, and re-layouts: 34.3 us -> none
    pallas_call x0 -> x4, Pallas kernels: none -> 24.5 us  [the longest x1 14.2 us: whiten(): pl.pallas_call(whiten_kernel, out_shape=jax.ShapeDtypeStruct((2, SUB * LA...]
    dot_general x6 -> x0, matrix products: 16.1 us -> none  [the longest x1 5.97 us: per_device(): left_part = jnp.dot(hidden, s_in, preferred_element_type=jnp.float32)]
    ppermute x0 -> x4, waiting for transfers between devices: none -> 13 us  [swap(): return lax.ppermute(x, 'tensor', [(i, i ^ bit) for i in range(tensor)])]
    all_to_all x0 -> x1, starting transfers between devices: none -> 12.4 us  [per_device(): lax.all_to_all(jnp.broadcast_to(both[None], (dp,) + both.shape), 'dp', 0, 0)]
  transfers between devices with their start and end apart: 2 -> 5, of which waited for: 2 -> 4; matrix products, arithmetic and copies ran while one was open for 0% -> 0% of each run, Pallas kernels for 0% -> 5%
where the time goes in v1:
time: 81.4 us; the launch traced here: 81 us
  Pallas kernels  24.5 us (30%)
  starting transfers between devices  23 us (28%)
  waiting for transfers between devices  21.2 us (26%)
  local copies, waits for them, and re-layouts  10.7 us (13%)
    pallas_call x1, Pallas kernels, whiten(): pl.pallas_call(whiten_kernel, out_shape=jax.ShapeDtypeStruct((2, SUB * LA...  14.2 us
    ppermute x4, waiting for transfers between devices, swap(): return lax.ppermute(x, 'tensor', [(i, i ^ bit) for i in range(tensor)])  13 us
    all_to_all x1, starting transfers between devices, per_device(): lax.all_to_all(jnp.broadcast_to(both[None], (dp,) + both.shape), 'dp', 0, 0)  12.4 us
    ppermute x4, starting transfers between devices, swap(): return lax.ppermute(x, 'tensor', [(i, i ^ bit) for i in range(tensor)])  10.6 us
    unnamed x22, local copies, waits for them, and re-layouts  10 us
    all_to_all x1, waiting for transfers between devices, per_device(): lax.all_to_all(jnp.broadcast_to(both[None], (dp,) + both.shape), 'dp', 0, 0)  8.26 us
    pallas_call x2, Pallas kernels, sketch(): pl.pallas_call(sketch_kernel, out_shape=jax.ShapeDtypeStruct((length // 2...  8.07 us
    pallas_call x1, Pallas kernels, outer(): pl.pallas_call(outer_kernel, out_shape=jax.ShapeDtypeStruct((SUB, LANES),...  2.27 us
  transfers between devices with their start and end apart: 5, of which 4 were waited for; matrix products, arithmetic and copies ran while one was open for 0% of the time, Pallas kernels for 5%

profile of v1, /device:TPU:1, one launch (start us, length us, event | category | flops | bytes accessed | tf_op | source)
XLA Modules:
  0.0 81.0 jit_solution(17011977447258227384)
XLA Ops:
  0.0 0.0 copy-start.4
  0.0 1.0 %copy.11.hid_table = bf16[8,128,32]{2,1,0:T(8,128)(2,1)S(1)} copy(bf16[8,128,32]{1,2,0:T(8,128)(2,1)} %param.15) | data formatting | bytes 131072 | tf_op args[5]
  1.0 1.0 %copy.12.out_table = bf16[8,128,32]{2,1,0:T(8,128)(2,1)S(1)} copy(bf16[8,128,32]{1,2,0:T(8,128)(2,1)} %param.18) | data formatting | bytes 131072 | tf_op args[8]
  2.1 0.0 copy-start
  2.1 3.1 %copy-done = bf16[1024,3584]{1,0:T(8,128)(2,1)S(1)} copy-done((bf16[1024,3584]{1,0:T(8,128)(2,1)S(1)}, bf16[1024,3584]{1,0:T(8,128)(2,1)}, u32[]{:S(2)}) %copy-start) | copy-done | bytes 7340056
  5.2 1.6 %copy-done.2 = bf16[1024,1024]{1,0:T(8,128)(2,1)S(1)} copy-done((bf16[1024,1024]{1,0:T(8,128)(2,1)S(1)}, bf16[1024,1024]{1,0:T(8,128)(2,1)}, u32[]{:S(2)}) %copy-start.2) | copy-done | bytes 2097176
  6.7 0.7 copy-done.3
  7.4 0.7 copy-done.5
  8.1 0.7 copy-done.6
  8.7 0.7 copy-done.7
  9.4 4.0 %sketch.3 = f32[256,128]{1,0:T(8,128)S(1)} custom-call(s32[1]{0:T(128)} %bitcast.2.which, s32[28]{0:T(128)S(1)} %copy-done.3, s32[28]{0:T(128)S(1)} %copy-done.5, s32[8]{0:T(128)S(1)} %copy-done.6, s32[8]{0:T(128)S(1)} %copy-done.7, bf16[8,128,32]{2,1,0:T(8,128)(2,1)S(1)} %copy.11.hid_table, bf16[8,128,32]{2,1,0:T(8,128)(2,1)S(1)} %copy.12.out_table, ...), custom_call_target="tpu_custom_call" | custom-call | tf_op jit(solution)/shard_map/sketch/pallas_call | solution.py:69
  13.4 2.6 %collective-permute-start = (f32[256,128]{1,0:T(8,128)S(1)}, f32[256,128]{1,0:T(8,128)S(1)}, u32[]{:S(2)}, u32[]{:S(2)}) collective-permute-start(f32[256,128]{1,0:T(8,128)S(1)} %sketch.3), channel_id=1, source_target_pairs={{0,1},{1,0},{2,3},{3,2},{4,5},{5,4},{6,7},{7,6},{8,9},{9,8},{10,11... | collective-permute-start | bytes 393224 | tf_op jit(solution)/shard_map/ppermute | solution.py:273
  16.0 0.0 copy-done.4
  16.0 0.0 copy-done.1
  16.0 4.0 %sketch.2 = f32[256,128]{1,0:T(8,128)S(1)} custom-call(s32[1]{0:T(128)} %bitcast.1.which, s32[28]{0:T(128)S(1)} %copy-done.4, s32[28]{0:T(128)S(1)} %copy-done.5, s32[8]{0:T(128)S(1)} %copy-done.6, s32[8]{0:T(128)S(1)} %copy-done.7, bf16[8,128,32]{2,1,0:T(8,128)(2,1)S(1)} %copy.11.hid_table, bf16[8,128,32]{2,1,0:T(8,128)(2,1)S(1)} %copy.12.out_table, ...), custom_call_target="tpu_custom_call" | custom-call | tf_op jit(solution)/shard_map/sketch/pallas_call | solution.py:69
  20.0 0.0 collective-permute-done
  20.1 3.1 %collective-permute-start.1 = (f32[256,128]{1,0:T(8,128)S(1)}, f32[256,128]{1,0:T(8,128)S(1)}, u32[]{:S(2)}, u32[]{:S(2)}) collective-permute-start(f32[256,128]{1,0:T(8,128)S(1)} %add.11), channel_id=1, source_target_pairs={{0,2},{1,3},{2,0},{3,1},{4,6},{5,7},{6,4},{7,5},{8,10},{9,11},{10,... | collective-permute-start | bytes 393224 | tf_op jit(solution)/shard_map/ppermute | solution.py:273
  23.1 6.7 %collective-permute-done.1 = f32[256,128]{1,0:T(8,128)S(1)} collective-permute-done((f32[256,128]{1,0:T(8,128)S(1)}, f32[256,128]{1,0:T(8,128)S(1)}, u32[]{:S(2)}, u32[]{:S(2)}) %collective-permute-start.1) | collective-permute-done | bytes 131104 | tf_op jit(solution)/shard_map/ppermute | solution.py:273
  29.9 0.0 copy-start.8
  29.9 5.0 %collective-permute-start.2 = (f32[256,128]{1,0:T(8,128)S(1)}, f32[256,128]{1,0:T(8,128)S(1)}, u32[]{:S(2)}, u32[]{:S(2)}) collective-permute-start(f32[256,128]{1,0:T(8,128)S(1)} %add.12.x_ref), channel_id=1, source_target_pairs={{0,4},{1,5},{2,6},{3,7},{4,0},{5,1},{6,2},{7,3},{8,12},{9,13},{10,... | collective-permute-start | bytes 393224 | tf_op jit(solution)/shard_map/ppermute | solution.py:273
  34.9 3.6 %collective-permute-done.2.other = f32[256,128]{1,0:T(8,128)S(1)} collective-permute-done((f32[256,128]{1,0:T(8,128)S(1)}, f32[256,128]{1,0:T(8,128)S(1)}, u32[]{:S(2)}, u32[]{:S(2)}) %collective-permute-start.2) | collective-permute-done | bytes 131104 | tf_op jit(solution)/shard_map/ppermute | solution.py:273
  38.5 0.0 copy-done.8
  38.5 0.6 copy-done.9
  39.1 2.3 %outer.1 = f32[8,128]{1,0:T(8,128)} custom-call(s32[1]{0:T(128)} %bitcast.1.which, s32[2]{0:T(128)} %lengths.1, f32[256,128]{1,0:T(8,128)} %copy-done.8, f32[256,128]{1,0:T(8,128)} %copy-done.9), custom_call_target="tpu_custom_call" | custom-call | tf_op jit(solution)/shard_map/outer/pallas_call | solution.py:116
  41.4 0.0 collective-permute-start.3
  41.4 2.7 %collective-permute-done.3 = f32[8,128]{1,0:T(8,128)S(1)} collective-permute-done((f32[8,128]{1,0:T(8,128)}, f32[8,128]{1,0:T(8,128)S(1)}, u32[]{:S(2)}, u32[]{:S(2)}) %collective-permute-start.3) | collective-permute-done | bytes 4128 | tf_op jit(solution)/shard_map/ppermute | solution.py:273
  44.1 0.7 pad_maximum_fusion
  44.7 0.7 broadcast_in_dim.2
  45.5 12.4 %all-to-all-start = ((f32[32,16,128]{2,1,0:T(8,128)}), f32[32,16,128]{2,1,0:T(8,128)S(1)}, u32[]{:S(2)}, u32[]{:S(2)}) async-start(f32[32,16,128]{2,1,0:T(8,128)} %broadcast_in_dim.2), calls=%async_computation | async-start | bytes 524288 | tf_op jit(solution)/shard_map/all_to_all | solution.py:280
  58.5 0.1 pad_add_fusion.place
  58.6 8.3 %all-to-all-done.gathered = f32[32,16,128]{2,1,0:T(8,128)S(1)} async-done(((f32[32,16,128]{2,1,0:T(8,128)}), f32[32,16,128]{2,1,0:T(8,128)S(1)}, u32[]{:S(2)}, u32[]{:S(2)}) %all-to-all-start) | async-done | bytes 262176 | tf_op jit(solution)/shard_map/all_to_all | solution.py:280
  66.9 14.2 %whiten.1 = f32[2,1024]{1,0:T(2,128)} custom-call(s32[2]{0:T(128)S(1)} %pad_add_fusion.place, f32[1]{0:T(128)S(6)} %copy.15.ridge, f32[32,16,128]{2,1,0:T(8,128)S(1)} %all-to-all-done.gathered), custom_call_target="tpu_custom_call" | custom-call | tf_op jit(solution)/shard_map/whiten/pallas_call | solution.py:244
  (9 shorter events, 0.0 us)
Async XLA Ops:
  0.0 16.0 %copy-start.4 = (s32[28]{0:T(128)S(1)}, s32[28]{0:T(128)}, u32[]{:S(2)}) copy-start(s32[28]{0:T(128)} %hid_kind.3) | copy-start | bytes 340
  2.1 3.1 %copy-start = (bf16[1024,3584]{1,0:T(8,128)(2,1)S(1)}, bf16[1024,3584]{1,0:T(8,128)(2,1)}, u32[]{:S(2)}) copy-start(bf16[1024,3584]{1,0:T(8,128)(2,1)} %hidden.3) | copy-start | bytes 22020100
  5.2 1.6 %copy-start.2 = (bf16[1024,1024]{1,0:T(8,128)(2,1)S(1)}, bf16[1024,1024]{1,0:T(8,128)(2,1)}, u32[]{:S(2)}) copy-start(bf16[1024,1024]{1,0:T(8,128)(2,1)} %out_grad.3) | copy-start | bytes 6291460
  6.7 0.7 copy-start.3
  7.4 0.7 copy-start.5
  8.1 0.7 copy-start.6
  8.7 0.7 copy-start.7
  9.4 6.6 %copy-start.1 = (bf16[1024,3584]{1,0:T(8,128)(2,1)S(1)}, bf16[1024,3584]{1,0:T(8,128)(2,1)}, u32[]{:S(2)}) copy-start(bf16[1024,3584]{1,0:T(8,128)(2,1)} %hidden.3) | copy-start | bytes 22020100
  13.4 6.6 %collective-permute-start = (f32[256,128]{1,0:T(8,128)S(1)}, f32[256,128]{1,0:T(8,128)S(1)}, u32[]{:S(2)}, u32[]{:S(2)}) collective-permute-start(f32[256,128]{1,0:T(8,128)S(1)} %sketch.3), channel_id=1, source_target_pairs={{0,1},{1,0},{2,3},{3,2},{4,5},{5,4},{6,7},{7,6},{8,9},{9,8},{10,11... | collective-permute-start | bytes 393224 | tf_op jit(solution)/shard_map/ppermute | solution.py:273
  20.1 9.8 %collective-permute-start.1 = (f32[256,128]{1,0:T(8,128)S(1)}, f32[256,128]{1,0:T(8,128)S(1)}, u32[]{:S(2)}, u32[]{:S(2)}) collective-permute-start(f32[256,128]{1,0:T(8,128)S(1)} %add.11), channel_id=1, source_target_pairs={{0,2},{1,3},{2,0},{3,1},{4,6},{5,7},{6,4},{7,5},{8,10},{9,11},{10,... | collective-permute-start | bytes 393224 | tf_op jit(solution)/shard_map/ppermute | solution.py:273
  29.9 8.6 %copy-start.8 = (f32[256,128]{1,0:T(8,128)}, f32[256,128]{1,0:T(8,128)S(1)}, u32[]{:S(2)}) copy-start(f32[256,128]{1,0:T(8,128)S(1)} %add.12.x_ref) | copy-start | bytes 393220
  29.9 8.6 %collective-permute-start.2 = (f32[256,128]{1,0:T(8,128)S(1)}, f32[256,128]{1,0:T(8,128)S(1)}, u32[]{:S(2)}, u32[]{:S(2)}) collective-permute-start(f32[256,128]{1,0:T(8,128)S(1)} %add.12.x_ref), channel_id=1, source_target_pairs={{0,4},{1,5},{2,6},{3,7},{4,0},{5,1},{6,2},{7,3},{8,12},{9,13},{10,... | collective-permute-start | bytes 393224 | tf_op jit(solution)/shard_map/ppermute | solution.py:273
  38.5 0.7 copy-start.9
  41.4 2.7 %collective-permute-start.3 = (f32[8,128]{1,0:T(8,128)}, f32[8,128]{1,0:T(8,128)S(1)}, u32[]{:S(2)}, u32[]{:S(2)}) collective-permute-start(f32[8,128]{1,0:T(8,128)} %outer.1), channel_id=1, source_target_pairs={{0,1},{1,0},{2,3},{3,2},{4,5},{5,4},{6,7},{7,6},{8,9},{9,8},{10,11... | collective-permute-start | bytes 12296 | tf_op jit(solution)/shard_map/ppermute | solution.py:273
  45.5 21.4 %all-to-all-start = ((f32[32,16,128]{2,1,0:T(8,128)}), f32[32,16,128]{2,1,0:T(8,128)S(1)}, u32[]{:S(2)}, u32[]{:S(2)}) async-start(f32[32,16,128]{2,1,0:T(8,128)} %broadcast_in_dim.2), calls=%async_computation | async-start | bytes 524288 | tf_op jit(solution)/shard_map/all_to_all | solution.py:280

commit v2 on v1

v2 whole, which is shorter than its diff:
```python
import functools

import jax
import jax.numpy as jnp
from jax import lax
from jax.experimental import pallas as pl
from jax.experimental.pallas import tpu as pltpu
from jax.sharding import PartitionSpec as P

F32 = jnp.float32
BF16 = jnp.bfloat16
LANES = 128
SUB = 8
VMEM = pl.BlockSpec(memory_space=pltpu.VMEM)
SMEM = pl.BlockSpec(memory_space=pltpu.SMEM)
HBM = pl.BlockSpec(memory_space=pl.ANY)


def iota(shape, dim):
    return lax.broadcasted_iota(jnp.int32, shape, dim)


def kept(z):
    return (z + 1) // 2 % 2


def sketch_kernel(
    away, hid_kind, hid_sign, out_kind, out_sign, hid_table, out_table, hidden, out_grad, x,
    hid_buf, out_buf, hid_tab, out_tab, hid_pick, hid_neg, out_pick, out_neg, s_in, s_out, small_sems, hid_sems, out_sem,
):
    which = kept(lax.axis_index("tensor"))
    which = 1 - which if away else which
    chunks, rows, depth = hid_buf.shape
    small = [
        pltpu.make_async_copy(src, dst, small_sems.at[n])
        for n, (src, dst) in enumerate(
            [
                (out_kind, out_pick),
                (out_sign, out_neg),
                (hid_kind, hid_pick),
                (hid_sign, hid_neg),
                (out_table, out_tab),
                (hid_table, hid_tab),
            ]
        )
    ]
    for copy in small:
        copy.start()
    here = pl.ds(pl.multiple_of(which * rows, rows), rows)
    out_copy = pltpu.make_async_copy(out_grad.at[here], out_buf, out_sem)
    out_copy.start()
    hid_copies = [
        pltpu.make_async_copy(hidden.at[here, pl.ds(c * depth, depth)], hid_buf.at[c], hid_sems.at[c])
        for c in range(chunks)
    ]
    for copy in hid_copies:
        copy.start()
    _, width, size = hid_tab.shape
    s_in[...] = jnp.zeros_like(s_in)
    s_out[...] = jnp.zeros_like(s_out)
    for copy in small:
        copy.wait()

    def fill(pick, neg, tab, s, row):
        for j in range(pick.shape[0]):
            block = tab[pick[j]]
            s[row : row + width, j * size : (j + 1) * size] = jnp.where(neg[j] > 0, block, -block)

    fill(out_pick, out_neg, out_tab, s_out, width)
    fill(hid_pick, hid_neg, hid_tab, s_in, 0)

    def times(left, right):
        return lax.dot_general(left, right, (((1,), (1,)), ((), ())), preferred_element_type=F32)

    out_copy.wait()
    total = times(out_buf[...], s_out[...])
    for c in range(chunks):
        hid_copies[c].wait()
        total += times(hid_buf[c], s_in[:, c * depth : (c + 1) * depth])
    half = rows // 2
    x[...] = total[:half] + pltpu.roll(total[half:], 2 * width, 1)


def sketch(away, hidden, out_grad, hid_kind, hid_sign, hid_table, out_kind, out_sign, out_table, length):
    deep, wide = hidden.shape[1], out_grad.shape[1]
    chunks = 7
    return pl.pallas_call(
        functools.partial(sketch_kernel, away),
        out_shape=jax.ShapeDtypeStruct((length // 2, LANES), F32),
        in_specs=[HBM] * 8,
        out_specs=VMEM,
        scratch_shapes=[
            pltpu.VMEM((chunks, length, deep // chunks), BF16),
            pltpu.VMEM((length, wide), BF16),
            pltpu.VMEM(hid_table.shape, BF16),
            pltpu.VMEM(out_table.shape, BF16),
            pltpu.SMEM(hid_kind.shape, jnp.int32),
            pltpu.SMEM(hid_sign.shape, jnp.int32),
            pltpu.SMEM(out_kind.shape, jnp.int32),
            pltpu.SMEM(out_sign.shape, jnp.int32),
            pltpu.VMEM((LANES, deep), BF16),
            pltpu.VMEM((LANES, wide), BF16),
            pltpu.SemaphoreType.DMA((6,)),
            pltpu.SemaphoreType.DMA((chunks,)),
            pltpu.SemaphoreType.DMA,
        ],
        compiler_params=pltpu.CompilerParams(vmem_limit_bytes=24 * 2**20),
        name="sketch_away" if away else "sketch_own",
    )(hid_kind, hid_sign, out_kind, out_sign, hid_table, out_table, hidden, out_grad)


def outer_kernel(lengths, x_ref, other, feats, counts, sem):
    copy = pltpu.make_async_copy(lengths, counts, sem)
    copy.start()
    x = x_ref[...] + other[...]
    half = x.shape[0]
    copy.wait()
    count = counts[kept(lax.axis_index("tensor"))]
    lane = iota(x.shape, 1)
    place = iota(x.shape, 0) + jnp.where(lane >= LANES // 2, half, 0)
    live = jnp.where(place < count, x, 0.0)
    z = lax.dot_general(
        live, x, (((0,), (0,)), ((), ())), precision=lax.Precision.HIGHEST, preferred_element_type=F32
    )
    row, column = iota((LANES, LANES), 0), iota((LANES, LANES), 1)
    spread = (row == column // 4).astype(F32)
    spread_later = (row - LANES // 2 == column // 4).astype(F32)
    quarter = LANES // 4
    y = jnp.dot(
        z[quarter : 2 * quarter], spread, precision=lax.Precision.HIGHEST, preferred_element_type=F32
    ) + jnp.dot(
        z[3 * quarter :], spread_later, precision=lax.Precision.HIGHEST, preferred_element_type=F32
    )
    own = iota((SUB, LANES), 1) % 4
    total = jnp.zeros((SUB, LANES), F32)
    for q in range(4):
        total += jnp.where(own == q, y[q * SUB : (q + 1) * SUB], 0.0)
    feats[...] = total * lax.rsqrt(jnp.full((SUB, LANES), count, jnp.int32).astype(F32))


def outer(lengths, x, other):
    return pl.pallas_call(
        outer_kernel,
        out_shape=jax.ShapeDtypeStruct((SUB, LANES), F32),
        in_specs=[HBM, VMEM, VMEM],
        out_specs=VMEM,
        scratch_shapes=[pltpu.SMEM(lengths.shape, jnp.int32), pltpu.SemaphoreType.DMA],
        name="outer",
    )(lengths, x, other)


def split(x, parts):
    out = []
    for _ in range(parts):
        piece = x.astype(BF16)
        out.append(piece)
        x = x - piece.astype(F32)
    return out


def whiten_kernel(ridge, gathered, out, aug, across, prods, ridge_here, sem):
    copy = pltpu.make_async_copy(ridge, ridge_here, sem)
    copy.start()
    seqs = gathered.shape[0]
    groups = seqs // SUB
    last = seqs // 2 - 1
    own = lax.axis_index("dp")
    for i in range(seqs):
        aug[i, seqs : seqs + SUB, :] = gathered[i]
    for h in range(2):
        aug[2 * own + h, seqs : seqs + SUB, :] = gathered[2 * last + h]
        aug[2 * last + h, seqs : seqs + SUB, :] = gathered[2 * own + h]
    for f in range(SUB):
        for j8 in range(groups):
            across[f, j8 * SUB : (j8 + 1) * SUB, :] = jnp.concatenate([aug[j8 * SUB + i, seqs + f : seqs + f + 1, :] for i in range(SUB)], axis=0)
    for f in range(SUB):
        aug[seqs + f, seqs : seqs + SUB, :] = jnp.zeros((SUB, LANES), F32)

    for i8 in range(groups):
        for i0 in range(0, SUB, 4):
            heads = [
                [jnp.broadcast_to(aug[i8 * SUB + ii, seqs + f : seqs + f + 1, :], (SUB, LANES)) for f in range(SUB)]
                for ii in range(i0, i0 + 4)
            ]
            for j8 in range(i8, groups):
                rows = [across[f, j8 * SUB : (j8 + 1) * SUB, :] for f in range(SUB)]
                for ii in range(4):
                    t = [heads[ii][f] * rows[f] for f in range(SUB)]
                    prods[i8 * SUB + i0 + ii, j8 * SUB : (j8 + 1) * SUB, :] = ((t[0] + t[1]) + (t[2] + t[3])) + (
                        (t[4] + t[5]) + (t[6] + t[7])
                    )
    before = (iota((LANES, LANES), 0) < iota((LANES, LANES), 1)).astype(BF16)
    for i8 in range(groups):
        wide = seqs - i8 * SUB
        block = prods[i8 * SUB : (i8 + 1) * SUB, i8 * SUB : seqs, :].reshape(SUB * wide, LANES)
        total = sum(jnp.dot(piece, before, preferred_element_type=F32) for piece in split(block, 3))
        aug[i8 * SUB : (i8 + 1) * SUB, i8 * SUB : seqs, :] = total.reshape(SUB, wide, LANES)
    copy.wait()
    r = ridge_here[0]
    sub = iota((SUB, LANES), 0)
    for i8 in range(groups):
        for ii in range(SUB):
            i = i8 * SUB + ii
            aug[i, i8 * SUB : (i8 + 1) * SUB, :] += jnp.where(sub == ii, r, 0.0)

    for p in range(groups):
        base = p * SUB
        diag = [aug[base + k, base : base + SUB, :] for k in range(SUB)]
        inv = []
        for k in range(SUB):
            inv.append(lax.rsqrt(diag[k][k : k + 1]))
            diag[k] = diag[k] * inv[k]
            for i in range(k + 1, SUB):
                diag[i] = diag[i] - diag[k][i : i + 1] * diag[k]
        for k in range(SUB):
            aug[base + k, base : base + SUB, :] = diag[k]
        for j8 in range(p + 1, groups + 1):
            rows = [aug[base + k, j8 * SUB : (j8 + 1) * SUB, :] for k in range(SUB)]
            for k in range(SUB):
                rows[k] = rows[k] * inv[k]
                for i in range(k + 1, SUB):
                    rows[i] = rows[i] - diag[k][i : i + 1] * rows[k]
            for k in range(SUB):
                aug[base + k, j8 * SUB : (j8 + 1) * SUB, :] = rows[k]

        for i8 in range(p + 1, groups + 1):
            for i0 in range(0, SUB, 4):
                heads = [
                    [jnp.broadcast_to(aug[base + k, i8 * SUB + ii : i8 * SUB + ii + 1, :], (SUB, LANES)) for k in range(SUB)]
                    for ii in range(i0, i0 + 4)
                ]
                for j8 in range(i8, groups + 1):
                    rows = [aug[base + k, j8 * SUB : (j8 + 1) * SUB, :] for k in range(SUB)]
                    for ii in range(4):
                        h = heads[ii]
                        i = i8 * SUB + i0 + ii
                        acc = aug[i, j8 * SUB : (j8 + 1) * SUB, :]
                        if 1:
                            t = [h[k] * rows[k] for k in range(SUB)]
                            acc = acc - (((t[0] + t[1]) + (t[2] + t[3])) + ((t[4] + t[5]) + (t[6] + t[7])))
                        else:
                            for k in range(SUB):
                                acc = acc - h[k] * rows[k]
                        aug[i, j8 * SUB : (j8 + 1) * SUB, :] = acc

    end = seqs - 1
    sol_end = aug[end, seqs : seqs + SUB, :] / aug[end, end : end + 1, :]
    sol = (aug[end - 1, seqs : seqs + SUB, :] - aug[end - 1, end : end + 1, :] * sol_end) / aug[
        end - 1, end - 1 : end, :
    ]
    x = [sol * r, sol_end * r]
    schur = [jnp.where(sub == f, r, 0.0) - r * aug[seqs + f, seqs : seqs + SUB, :] for f in range(SUB)]
    w = [jnp.zeros((SUB, LANES), F32) for _ in range(2)]
    for f in range(SUB):
        scale = lax.rsqrt(schur[f][f : f + 1])
        line = schur[f] * scale
        for i in range(f + 1, SUB):
            schur[i] = schur[i] - line[i : i + 1] * line
        for h in range(2):
            value = x[h][f : f + 1] * scale
            w[h] = jnp.where(sub == f, value, w[h])
            x[h] = x[h] - line * value
    size = SUB * LANES
    w = jnp.concatenate(w, axis=0) * jnp.sqrt(jnp.full((2 * SUB, LANES), size, F32))
    spread = (iota((LANES, size), 0) == iota((LANES, size), 1) // SUB).astype(BF16)
    wide = sum(jnp.dot(piece, spread, preferred_element_type=F32) for piece in split(w, 3))
    wide = jnp.where(iota((2 * SUB, size), 1) % SUB == iota((2 * SUB, size), 0) % SUB, wide, 0.0)
    lines = [jnp.sum(wide[h * SUB : (h + 1) * SUB], axis=0, keepdims=True) for h in range(2)]
    swap = kept(lax.axis_index("tensor") // 2 * 2) > 0
    out[0:1, :] = jnp.where(swap, lines[1], lines[0])
    out[1:2, :] = jnp.where(swap, lines[0], lines[1])


def whiten(ridge, gathered):
    seqs = gathered.shape[0]
    return pl.pallas_call(
        whiten_kernel,
        out_shape=jax.ShapeDtypeStruct((2, SUB * LANES), F32),
        in_specs=[HBM, VMEM],
        out_specs=VMEM,
        scratch_shapes=[
            pltpu.VMEM((seqs + SUB, seqs + SUB, LANES), F32),
            pltpu.VMEM((SUB, seqs, LANES), F32),
            pltpu.VMEM((seqs, seqs, LANES), F32),
            pltpu.SMEM(ridge.shape, F32),
            pltpu.SemaphoreType.DMA,
        ],
        compiler_params=pltpu.CompilerParams(vmem_limit_bytes=24 * 2**20),
        name="whiten",
    )(ridge, gathered)


def per_device(
    dp, tensor,
    hidden, out_grad, lengths, hid_kind, hid_sign, hid_table, out_kind, out_sign, out_table, ridge
):
    length = hidden.shape[0] // lengths.shape[0]

    def of(away):
        return sketch(
            away, hidden, out_grad, hid_kind, hid_sign, hid_table.swapaxes(1, 2),
            out_kind, out_sign, out_table.swapaxes(1, 2), length,
        )

    def swap(x, other):
        return lax.ppermute(x, "tensor", [(i, other(i) % tensor) for i in range(tensor)])

    x = of(True)
    x = of(False) + swap(x, lambda i: i ^ 1)
    x = x + swap(x, lambda i: i + 1 if i % 2 else i - 1)
    feats = outer(lengths, x, swap(x, lambda i: i - 3 if i % 2 else i + 3))
    groups = [[d * tensor + z + h for d in range(dp) for h in range(2)] for z in range(0, tensor, 2)]
    sent = jnp.broadcast_to(feats[None], (2 * dp,) + feats.shape)
    gathered = lax.all_to_all(sent, ("dp", "tensor"), 0, 0, axis_index_groups=groups)
    return whiten(ridge, gathered)


def solution(mesh):
    return jax.shard_map(
        functools.partial(per_device, mesh.shape["dp"], mesh.shape["tensor"]),
        mesh=mesh,
        in_specs=(
            P("dp", "tensor"),
            P("dp", "tensor"),
            P("dp"),
            P("tensor"),
            P("tensor"),
            P(),
            P("tensor"),
            P("tensor"),
            P(),
            P(),
        ),
        out_specs=P("dp", None),
        check_vma=False,
    )
```

time: 81.4 us -> 63.9 us (0.79)
  Pallas kernels: 24.5 us -> 15.7 us
  starting transfers between devices: 23 us -> 18.8 us
  waiting for transfers between devices: 21.2 us -> 17.2 us
    pallas_call x1, Pallas kernels: 14.2 us -> 4.82 us  [whiten(): pl.pallas_call(whiten_kernel, out_shape=jax.ShapeDtypeStruct((2, SUB * LA...]
    ppermute x4 -> x3, waiting for transfers between devices: 13 us -> 8.23 us  [swap(): lax.ppermute(x, 'tensor', [(i, other(i) % tensor) for i in range(tensor)])]
    all_to_all x1, starting transfers between devices: 12.4 us -> 9.76 us  [per_device(): lax.all_to_all(sent, ('dp', 'tensor'), 0, 0, axis_index_groups=groups)]
    ppermute x4 -> x3, starting transfers between devices: 10.6 us -> 9.03 us  [swap(): lax.ppermute(x, 'tensor', [(i, other(i) % tensor) for i in range(tensor)])]
    unnamed x22 -> x20, local copies, waits for them, and re-layouts: 10 us -> 9.62 us
  transfers between devices with their start and end apart: 5 -> 4, of which waited for: 4 -> 3; matrix products, arithmetic and copies ran while one was open for 0% -> 0% of each run, Pallas kernels for 5% -> 6%
where the time goes in v2:
time: 63.9 us; the launch traced here: 63.5 us
  starting transfers between devices  18.8 us (29%)
  waiting for transfers between devices  17.2 us (27%)
  Pallas kernels  15.7 us (25%)
  local copies, waits for them, and re-layouts  11 us (17%)
  between operations  0.72 us (1%)
    all_to_all x1, starting transfers between devices, per_device(): lax.all_to_all(sent, ('dp', 'tensor'), 0, 0, axis_index_groups=groups)  9.76 us
    unnamed x20, local copies, waits for them, and re-layouts  9.62 us
    ppermute x3, starting transfers between devices, swap(): lax.ppermute(x, 'tensor', [(i, other(i) % tensor) for i in range(tensor)])  9.03 us
    all_to_all x1, waiting for transfers between devices, per_device(): lax.all_to_all(sent, ('dp', 'tensor'), 0, 0, axis_index_groups=groups)  8.97 us
    ppermute x3, waiting for transfers between devices, swap(): lax.ppermute(x, 'tensor', [(i, other(i) % tensor) for i in range(tensor)])  8.23 us
    pallas_call x2, Pallas kernels, sketch(): pl.pallas_call(functools.partial(sketch_kernel, away), out_shape=jax.Shap...  7.96 us
    pallas_call x1, Pallas kernels, whiten(): pl.pallas_call(whiten_kernel, out_shape=jax.ShapeDtypeStruct((2, SUB * LA...  4.82 us
    pallas_call x1, Pallas kernels, outer(): pl.pallas_call(outer_kernel, out_shape=jax.ShapeDtypeStruct((SUB, LANES),...  2.94 us
  transfers between devices with their start and end apart: 4, of which 3 were waited for; matrix products, arithmetic and copies ran while one was open for 0% of the time, Pallas kernels for 6%

profile of v2, /device:TPU:1, one launch (start us, length us, event | category | flops | bytes accessed | tf_op | source)
XLA Modules:
  0.0 63.5 jit_solution(10833544978705588930)
XLA Ops:
  0.0 0.0 copy-start
  0.0 3.1 %copy-done = bf16[1024,3584]{1,0:T(8,128)(2,1)S(1)} copy-done((bf16[1024,3584]{1,0:T(8,128)(2,1)S(1)}, bf16[1024,3584]{1,0:T(8,128)(2,1)}, u32[]{:S(2)}) %copy-start) | copy-done | bytes 7340056
  3.1 0.0 copy-start.1
  3.1 1.6 %copy-done.1 = bf16[1024,1024]{1,0:T(8,128)(2,1)S(1)} copy-done((bf16[1024,1024]{1,0:T(8,128)(2,1)S(1)}, bf16[1024,1024]{1,0:T(8,128)(2,1)}, u32[]{:S(2)}) %copy-start.1) | copy-done | bytes 2097176
  4.7 0.0 copy-start.2
  4.7 0.8 %copy-done.2 = bf16[8,128,32]{1,2,0:T(8,128)(2,1)S(1)} copy-done((bf16[8,128,32]{1,2,0:T(8,128)(2,1)S(1)}, bf16[8,128,32]{1,2,0:T(8,128)(2,1)}, u32[]{:S(2)}) %copy-start.2) | copy-done | bytes 65560
  5.5 0.0 copy-start.3
  5.5 0.8 %copy-done.3 = bf16[8,128,32]{1,2,0:T(8,128)(2,1)S(1)} copy-done((bf16[8,128,32]{1,2,0:T(8,128)(2,1)S(1)}, bf16[8,128,32]{1,2,0:T(8,128)(2,1)}, u32[]{:S(2)}) %copy-start.3) | copy-done | bytes 65560
  6.4 0.0 copy-start.4
  6.4 0.7 %copy-done.4 = s32[28]{0:T(128)S(1)} copy-done((s32[28]{0:T(128)S(1)}, s32[28]{0:T(128)}, u32[]{:S(2)}) %copy-start.4) | copy-done | bytes 136
  7.0 0.0 copy-start.5
  7.0 0.7 %copy-done.5 = s32[28]{0:T(128)S(1)} copy-done((s32[28]{0:T(128)S(1)}, s32[28]{0:T(128)}, u32[]{:S(2)}) %copy-start.5) | copy-done | bytes 136
  7.7 0.0 copy-start.6
  7.7 0.7 %copy-done.6 = s32[8]{0:T(128)S(1)} copy-done((s32[8]{0:T(128)S(1)}, s32[8]{0:T(128)}, u32[]{:S(2)}) %copy-start.6) | copy-done | bytes 56
  8.3 0.7 %copy-done.7 = s32[8]{0:T(128)S(1)} copy-done((s32[8]{0:T(128)S(1)}, s32[8]{0:T(128)}, u32[]{:S(2)}) %copy-start.7) | copy-done | bytes 56
  9.0 4.0 %sketch_away.1 = f32[256,128]{1,0:T(8,128)S(1)} custom-call(s32[28]{0:T(128)S(1)} %copy-done.4, s32[28]{0:T(128)S(1)} %copy-done.5, s32[8]{0:T(128)S(1)} %copy-done.6, s32[8]{0:T(128)S(1)} %copy-done.7, bf16[8,32,128]{2,1,0:T(8,128)(2,1)S(1)} %bitcast.2, bf16[8,32,128]{2,1,0:T(8,128)(2,1)S(1)} %bitcast.4, bf16[1024,3584]{1,0:T(8,128)(2,1)S(1)} %copy-done, ...), custom_call_target="tpu_custom_call" | custom-call | tf_op jit(solution)/shard_map/sketch_away/pallas_call | solution.py:87
  13.0 2.6 %collective-permute-start = (f32[256,128]{1,0:T(8,128)S(1)}, f32[256,128]{1,0:T(8,128)S(1)}, u32[]{:S(2)}, u32[]{:S(2)}) collective-permute-start(f32[256,128]{1,0:T(8,128)S(1)} %sketch_away.1), channel_id=1, source_target_pairs={{0,1},{1,0},{2,3},{3,2},{4,5},{5,4},{6,7},{7,6},{8,9},{9,8},{10,11... | collective-permute-start | bytes 393224 | tf_op jit(solution)/shard_map/ppermute | solution.py:306
  15.5 4.0 %sketch_own.1 = f32[256,128]{1,0:T(8,128)S(1)} custom-call(s32[28]{0:T(128)S(1)} %copy-done.4, s32[28]{0:T(128)S(1)} %copy-done.5, s32[8]{0:T(128)S(1)} %copy-done.6, s32[8]{0:T(128)S(1)} %copy-done.7, bf16[8,32,128]{2,1,0:T(8,128)(2,1)S(1)} %bitcast.3, bf16[8,32,128]{2,1,0:T(8,128)(2,1)S(1)} %bitcast.5, bf16[1024,3584]{1,0:T(8,128)(2,1)S(1)} %copy-done, ...), custom_call_target="tpu_custom_call" | custom-call | tf_op jit(solution)/shard_map/sketch_own/pallas_call | solution.py:87
  19.5 0.0 collective-permute-done
  19.5 4.8 %collective-permute-start.1 = (f32[256,128]{1,0:T(8,128)S(1)}, f32[256,128]{1,0:T(8,128)S(1)}, u32[]{:S(2)}, u32[]{:S(2)}) collective-permute-start(f32[256,128]{1,0:T(8,128)S(1)} %add.6), channel_id=1, source_target_pairs={{0,7},{1,2},{2,1},{3,4},{4,3},{5,6},{6,5},{7,0},{8,15},{9,10},{10,... | collective-permute-start | bytes 393224 | tf_op jit(solution)/shard_map/ppermute | solution.py:306
  24.3 2.4 %collective-permute-done.1 = f32[256,128]{1,0:T(8,128)S(1)} collective-permute-done((f32[256,128]{1,0:T(8,128)S(1)}, f32[256,128]{1,0:T(8,128)S(1)}, u32[]{:S(2)}, u32[]{:S(2)}) %collective-permute-start.1) | collective-permute-done | bytes 131104 | tf_op jit(solution)/shard_map/ppermute | solution.py:306
  26.7 0.0 copy-start.8
  26.7 1.7 %collective-permute-start.2 = (f32[256,128]{1,0:T(8,128)S(1)}, f32[256,128]{1,0:T(8,128)S(1)}, u32[]{:S(2)}, u32[]{:S(2)}) collective-permute-start(f32[256,128]{1,0:T(8,128)S(1)} %add.7.x_ref), channel_id=1, source_target_pairs={{0,3},{1,6},{2,5},{3,0},{4,7},{5,2},{6,1},{7,4},{8,11},{9,14},{10,... | collective-permute-start | bytes 393224 | tf_op jit(solution)/shard_map/ppermute | solution.py:306
  28.4 5.9 %collective-permute-done.2.other = f32[256,128]{1,0:T(8,128)S(1)} collective-permute-done((f32[256,128]{1,0:T(8,128)S(1)}, f32[256,128]{1,0:T(8,128)S(1)}, u32[]{:S(2)}, u32[]{:S(2)}) %collective-permute-start.2) | collective-permute-done | bytes 131104 | tf_op jit(solution)/shard_map/ppermute | solution.py:306
  34.3 0.0 copy-done.8
  34.3 0.0 copy-start.9
  34.3 0.6 %copy-done.9 = f32[256,128]{1,0:T(8,128)} copy-done((f32[256,128]{1,0:T(8,128)}, f32[256,128]{1,0:T(8,128)S(1)}, u32[]{:S(2)}) %copy-start.9) | copy-done | bytes 131096
  34.9 2.9 %outer.1 = f32[8,128]{1,0:T(8,128)} custom-call(s32[2]{0:T(128)} %lengths.1, f32[256,128]{1,0:T(8,128)} %copy-done.8, f32[256,128]{1,0:T(8,128)} %copy-done.9), custom_call_target="tpu_custom_call" | custom-call | tf_op jit(solution)/shard_map/outer/pallas_call | solution.py:142
  37.9 1.4 %broadcast_in_dim.2 = f32[64,8,128]{2,1,0:T(8,128)} broadcast(f32[8,128]{1,0:T(8,128)} %outer.1), dimensions={1,2} | broadcast | bytes 266240 | tf_op jit(solution)/shard_map/broadcast_in_dim | solution.py:313
  39.3 9.8 %all-to-all-start = ((f32[64,8,128]{2,1,0:T(8,128)}), f32[64,8,128]{2,1,0:T(8,128)S(1)}, u32[]{:S(2)}, u32[]{:S(2)}) async-start(f32[64,8,128]{2,1,0:T(8,128)} %broadcast_in_dim.2), calls=%async_computation | async-start | bytes 524288 | tf_op jit(solution)/shard_map/all_to_all | solution.py:314
  49.7 9.0 %all-to-all-done.gathered = f32[64,8,128]{2,1,0:T(8,128)S(1)} async-done(((f32[64,8,128]{2,1,0:T(8,128)}), f32[64,8,128]{2,1,0:T(8,128)S(1)}, u32[]{:S(2)}, u32[]{:S(2)}) %all-to-all-start) | async-done | bytes 262176 | tf_op jit(solution)/shard_map/all_to_all | solution.py:314
  58.7 4.8 %whiten.1 = f32[2,1024]{1,0:T(2,128)} custom-call(f32[1]{0:T(128)S(6)} %copy.11.ridge, f32[64,8,128]{2,1,0:T(8,128)S(1)} %all-to-all-done.gathered), custom_call_target="tpu_custom_call" | custom-call | tf_op jit(solution)/shard_map/whiten/pallas_call | solution.py:276
  (3 shorter events, 0.0 us)
Async XLA Ops:
  0.0 3.1 %copy-start = (bf16[1024,3584]{1,0:T(8,128)(2,1)S(1)}, bf16[1024,3584]{1,0:T(8,128)(2,1)}, u32[]{:S(2)}) copy-start(bf16[1024,3584]{1,0:T(8,128)(2,1)} %hidden.3) | copy-start | bytes 22020100
  3.1 1.6 %copy-start.1 = (bf16[1024,1024]{1,0:T(8,128)(2,1)S(1)}, bf16[1024,1024]{1,0:T(8,128)(2,1)}, u32[]{:S(2)}) copy-start(bf16[1024,1024]{1,0:T(8,128)(2,1)} %out_grad.3) | copy-start | bytes 6291460
  4.7 0.8 %copy-start.2 = (bf16[8,128,32]{1,2,0:T(8,128)(2,1)S(1)}, bf16[8,128,32]{1,2,0:T(8,128)(2,1)}, u32[]{:S(2)}) copy-start(bf16[8,128,32]{1,2,0:T(8,128)(2,1)} %param.15) | copy-start | bytes 196612
  5.5 0.8 %copy-start.3 = (bf16[8,128,32]{1,2,0:T(8,128)(2,1)S(1)}, bf16[8,128,32]{1,2,0:T(8,128)(2,1)}, u32[]{:S(2)}) copy-start(bf16[8,128,32]{1,2,0:T(8,128)(2,1)} %param.18) | copy-start | bytes 196612
  6.4 0.7 %copy-start.4 = (s32[28]{0:T(128)S(1)}, s32[28]{0:T(128)}, u32[]{:S(2)}) copy-start(s32[28]{0:T(128)} %hid_kind.3) | copy-start | bytes 340
  7.0 0.7 %copy-start.5 = (s32[28]{0:T(128)S(1)}, s32[28]{0:T(128)}, u32[]{:S(2)}) copy-start(s32[28]{0:T(128)} %hid_sign.3) | copy-start | bytes 340
  7.7 0.7 %copy-start.6 = (s32[8]{0:T(128)S(1)}, s32[8]{0:T(128)}, u32[]{:S(2)}) copy-start(s32[8]{0:T(128)} %out_kind.3) | copy-start | bytes 100
  8.3 0.7 %copy-start.7 = (s32[8]{0:T(128)S(1)}, s32[8]{0:T(128)}, u32[]{:S(2)}) copy-start(s32[8]{0:T(128)} %out_sign.3) | copy-start | bytes 100
  13.0 6.5 %collective-permute-start = (f32[256,128]{1,0:T(8,128)S(1)}, f32[256,128]{1,0:T(8,128)S(1)}, u32[]{:S(2)}, u32[]{:S(2)}) collective-permute-start(f32[256,128]{1,0:T(8,128)S(1)} %sketch_away.1), channel_id=1, source_target_pairs={{0,1},{1,0},{2,3},{3,2},{4,5},{5,4},{6,7},{7,6},{8,9},{9,8},{10,11... | collective-permute-start | bytes 393224 | tf_op jit(solution)/shard_map/ppermute | solution.py:306
  19.5 7.1 %collective-permute-start.1 = (f32[256,128]{1,0:T(8,128)S(1)}, f32[256,128]{1,0:T(8,128)S(1)}, u32[]{:S(2)}, u32[]{:S(2)}) collective-permute-start(f32[256,128]{1,0:T(8,128)S(1)} %add.6), channel_id=1, source_target_pairs={{0,7},{1,2},{2,1},{3,4},{4,3},{5,6},{6,5},{7,0},{8,15},{9,10},{10,... | collective-permute-start | bytes 393224 | tf_op jit(solution)/shard_map/ppermute | solution.py:306
  26.7 7.6 %copy-start.8 = (f32[256,128]{1,0:T(8,128)}, f32[256,128]{1,0:T(8,128)S(1)}, u32[]{:S(2)}) copy-start(f32[256,128]{1,0:T(8,128)S(1)} %add.7.x_ref) | copy-start | bytes 393220
  26.7 7.6 %collective-permute-start.2 = (f32[256,128]{1,0:T(8,128)S(1)}, f32[256,128]{1,0:T(8,128)S(1)}, u32[]{:S(2)}, u32[]{:S(2)}) collective-permute-start(f32[256,128]{1,0:T(8,128)S(1)} %add.7.x_ref), channel_id=1, source_target_pairs={{0,3},{1,6},{2,5},{3,0},{4,7},{5,2},{6,1},{7,4},{8,11},{9,14},{10,... | collective-permute-start | bytes 393224 | tf_op jit(solution)/shard_map/ppermute | solution.py:306
  34.3 0.7 %copy-start.9 = (f32[256,128]{1,0:T(8,128)}, f32[256,128]{1,0:T(8,128)S(1)}, u32[]{:S(2)}) copy-start(f32[256,128]{1,0:T(8,128)S(1)} %collective-permute-done.2.other) | copy-start | bytes 393220
  39.3 19.4 %all-to-all-start = ((f32[64,8,128]{2,1,0:T(8,128)}), f32[64,8,128]{2,1,0:T(8,128)S(1)}, u32[]{:S(2)}, u32[]{:S(2)}) async-start(f32[64,8,128]{2,1,0:T(8,128)} %broadcast_in_dim.2), calls=%async_computation | async-start | bytes 524288 | tf_op jit(solution)/shard_map/all_to_all | solution.py:314

commit v3 on v2

--- a/solution.py
+++ b/solution.py
@@ -13,7 +13,7 @@
 SUB = 8
 VMEM = pl.BlockSpec(memory_space=pltpu.VMEM)
 SMEM = pl.BlockSpec(memory_space=pltpu.SMEM)
-HBM = pl.BlockSpec(memory_space=pl.ANY)
+HBM = pl.BlockSpec(memory_space=pltpu.HBM)
 
 
 def iota(shape, dim):
@@ -56,29 +56,27 @@
     for copy in hid_copies:
         copy.start()
     _, width, size = hid_tab.shape
-    s_in[...] = jnp.zeros_like(s_in)
-    s_out[...] = jnp.zeros_like(s_out)
     for copy in small:
         copy.wait()
 
-    def fill(pick, neg, tab, s, row):
+    def fill(pick, neg, tab, s):
         for j in range(pick.shape[0]):
             block = tab[pick[j]]
-            s[row : row + width, j * size : (j + 1) * size] = jnp.where(neg[j] > 0, block, -block)
-
-    fill(out_pick, out_neg, out_tab, s_out, width)
-    fill(hid_pick, hid_neg, hid_tab, s_in, 0)
+            s[:, j * size : (j + 1) * size] = jnp.where(neg[j] > 0, block, -block)
 
     def times(left, right):
         return lax.dot_general(left, right, (((1,), (1,)), ((), ())), preferred_element_type=F32)
 
+    fill(out_pick, out_neg, out_tab, s_out)
+    fill(hid_pick, hid_neg, hid_tab, s_in)
     out_copy.wait()
-    total = times(out_buf[...], s_out[...])
+    x[width:, :] = times(s_out[...], out_buf[...])
+    total = None
     for c in range(chunks):
         hid_copies[c].wait()
-        total += times(hid_buf[c], s_in[:, c * depth : (c + 1) * depth])
-    half = rows // 2
-    x[...] = total[:half] + pltpu.roll(total[half:], 2 * width, 1)
+        part = times(s_in[:, c * depth : (c + 1) * depth], hid_buf[c])
+        total = part if total is None else total + part
+    x[:width, :] = total
 
 
 def sketch(away, hidden, out_grad, hid_kind, hid_sign, hid_table, out_kind, out_sign, out_table, length):
@@ -86,7 +84,7 @@
     chunks = 7
     return pl.pallas_call(
         functools.partial(sketch_kernel, away),
-        out_shape=jax.ShapeDtypeStruct((length // 2, LANES), F32),
+        out_shape=jax.ShapeDtypeStruct((2 * hid_table.shape[1], length), F32),
         in_specs=[HBM] * 8,
         out_specs=VMEM,
         scratch_shapes=[
@@ -98,55 +96,15 @@
             pltpu.SMEM(hid_sign.shape, jnp.int32),
             pltpu.SMEM(out_kind.shape, jnp.int32),
             pltpu.SMEM(out_sign.shape, jnp.int32),
-            pltpu.VMEM((LANES, deep), BF16),
-            pltpu.VMEM((LANES, wide), BF16),
+            pltpu.VMEM((hid_table.shape[1], deep), BF16),
+            pltpu.VMEM((out_table.shape[1], wide), BF16),
             pltpu.SemaphoreType.DMA((6,)),
             pltpu.SemaphoreType.DMA((chunks,)),
             pltpu.SemaphoreType.DMA,
         ],
         compiler_params=pltpu.CompilerParams(vmem_limit_bytes=24 * 2**20),
         name="sketch_away" if away else "sketch_own",
-    )(hid_kind, hid_sign, out_kind, out_sign, hid_table, out_table, hidden, out_grad)
-
-
-def outer_kernel(lengths, x_ref, other, feats, counts, sem):
-    copy = pltpu.make_async_copy(lengths, counts, sem)
-    copy.start()
-    x = x_ref[...] + other[...]
-    half = x.shape[0]
-    copy.wait()
-    count = counts[kept(lax.axis_index("tensor"))]
-    lane = iota(x.shape, 1)
-    place = iota(x.shape, 0) + jnp.where(lane >= LANES // 2, half, 0)
-    live = jnp.where(place < count, x, 0.0)
-    z = lax.dot_general(
-        live, x, (((0,), (0,)), ((), ())), precision=lax.Precision.HIGHEST, preferred_element_type=F32
-    )
-    row, column = iota((LANES, LANES), 0), iota((LANES, LANES), 1)
-    spread = (row == column // 4).astype(F32)
-    spread_later = (row - LANES // 2 == column // 4).astype(F32)
-    quarter = LANES // 4
-    y = jnp.dot(
-        z[quarter : 2 * quarter], spread, precision=lax.Precision.HIGHEST, preferred_element_type=F32
-    ) + jnp.dot(
-        z[3 * quarter :], spread_later, precision=lax.Precision.HIGHEST, preferred_element_type=F32
-    )
-    own = iota((SUB, LANES), 1) % 4
-    total = jnp.zeros((SUB, LANES), F32)
-    for q in range(4):
-        total += jnp.where(own == q, y[q * SUB : (q + 1) * SUB], 0.0)
-    feats[...] = total * lax.rsqrt(jnp.full((SUB, LANES), count, jnp.int32).astype(F32))
-
-
-def outer(lengths, x, other):
-    return pl.pallas_call(
-        outer_kernel,
-        out_shape=jax.ShapeDtypeStruct((SUB, LANES), F32),
-        in_specs=[HBM, VMEM, VMEM],
-        out_specs=VMEM,
-        scratch_shapes=[pltpu.SMEM(lengths.shape, jnp.int32), pltpu.SemaphoreType.DMA],
-        name="outer",
-    )(lengths, x, other)
+    )(*[pltpu.with_memory_space_constraint(v, pltpu.HBM) for v in (hid_kind, hid_sign, out_kind, out_sign, hid_table, out_table, hidden, out_grad)])
 
 
 def split(x, parts):
@@ -156,6 +114,40 @@
         out.append(piece)
         x = x - piece.astype(F32)
     return out
+
+
+def outer_kernel(lengths, x_ref, other, feats, counts, sem):
+    copy = pltpu.make_async_copy(lengths, counts, sem)
+    copy.start()
+    x = x_ref[...] + other[...]
+    width = x.shape[0] // 2
+    copy.wait()
+    count = counts[kept(lax.axis_index("tensor"))]
+    a = jnp.where(iota((width, x.shape[1]), 1) < count, x[:width], 0.0)
+    a = jnp.concatenate(split(a, 2), axis=0)
+    b = jnp.concatenate(split(x[width:], 2), axis=0)
+    z = lax.dot_general(b, a, (((1,), (1,)), ((), ())), preferred_element_type=F32)
+    z = z[:width] + z[width:]
+    spread = (iota((2 * width, LANES), 0) % width == iota((2 * width, LANES), 1) // 4).astype(BF16)
+    y = sum(jnp.dot(piece, spread, preferred_element_type=F32) for piece in split(z, 3))
+    own = iota((SUB, LANES), 1) % 4
+    total = jnp.zeros((SUB, LANES), F32)
+    for q in range(4):
+        total += jnp.where(own == q, y[q * SUB : (q + 1) * SUB], 0.0)
+    total *= lax.rsqrt(jnp.full((SUB, LANES), count, jnp.int32).astype(F32))
+    for n in range(feats.shape[0]):
+        feats[n] = total
+
+
+def outer(lengths, x, other, takers):
+    return pl.pallas_call(
+        outer_kernel,
+        out_shape=jax.ShapeDtypeStruct((takers, SUB, LANES), F32),
+        in_specs=[HBM, VMEM, VMEM],
+        out_specs=VMEM,
+        scratch_shapes=[pltpu.SMEM(lengths.shape, jnp.int32), pltpu.SemaphoreType.DMA],
+        name="outer",
+    )(lengths, x, other)
 
 
 def whiten_kernel(ridge, gathered, out, aug, across, prods, ridge_here, sem):
@@ -308,10 +300,9 @@
     x = of(True)
     x = of(False) + swap(x, lambda i: i ^ 1)
     x = x + swap(x, lambda i: i + 1 if i % 2 else i - 1)
-    feats = outer(lengths, x, swap(x, lambda i: i - 3 if i % 2 else i + 3))
+    feats = outer(lengths, x, swap(x, lambda i: i - 3 if i % 2 else i + 3), 2 * dp)
     groups = [[d * tensor + z + h for d in range(dp) for h in range(2)] for z in range(0, tensor, 2)]
-    sent = jnp.broadcast_to(feats[None], (2 * dp,) + feats.shape)
-    gathered = lax.all_to_all(sent, ("dp", "tensor"), 0, 0, axis_index_groups=groups)
+    gathered = lax.all_to_all(feats, ("dp", "tensor"), 0, 0, axis_index_groups=groups)
     return whiten(ridge, gathered)
 
 

time: 63.9 us -> 54.2 us (0.85)
  local copies, waits for them, and re-layouts: 11 us -> 0.65 us
  waiting for transfers between devices: 17.2 us -> 18.9 us
  starting transfers between devices: 18.8 us -> 18.1 us
    unnamed x20 -> x4, local copies, waits for them, and re-layouts: 9.62 us -> 0.65 us
    ppermute x3, waiting for transfers between devices: 8.23 us -> 9.98 us  [swap(): lax.ppermute(x, 'tensor', [(i, other(i) % tensor) for i in range(tensor)])]
    broadcast_in_dim x1 -> x0, local copies, waits for them, and re-layouts: 1.41 us -> none  [per_device(): sent = jnp.broadcast_to(feats[None], (2 * dp,) + feats.shape)]
  transfers between devices with their start and end apart: 4 -> 4, of which waited for: 3 -> 3; matrix products, arithmetic and copies ran while one was open for 0% -> 0% of each run, Pallas kernels for 6% -> 8%
where the time goes in v3:
time: 54.2 us; the launch traced here: 54 us
  waiting for transfers between devices  18.9 us (35%)
  starting transfers between devices  18.1 us (33%)
  Pallas kernels  15.6 us (29%)
  between operations  0.71 us (1%)
  local copies, waits for them, and re-layouts  0.65 us (1%)
    ppermute x3, waiting for transfers between devices, swap(): lax.ppermute(x, 'tensor', [(i, other(i) % tensor) for i in range(tensor)])  9.98 us
    all_to_all x1, starting transfers between devices, per_device(): lax.all_to_all(feats, ('dp', 'tensor'), 0, 0, axis_index_groups=groups)  9.45 us
    all_to_all x1, waiting for transfers between devices, per_device(): lax.all_to_all(feats, ('dp', 'tensor'), 0, 0, axis_index_groups=groups)  8.97 us
    ppermute x3, starting transfers between devices, swap(): lax.ppermute(x, 'tensor', [(i, other(i) % tensor) for i in range(tensor)])  8.63 us
    pallas_call x2, Pallas kernels, sketch(): pl.pallas_call(functools.partial(sketch_kernel, away), out_shape=jax.Shap...  8.12 us
    pallas_call x1, Pallas kernels, whiten(): pl.pallas_call(whiten_kernel, out_shape=jax.ShapeDtypeStruct((2, SUB * LA...  4.82 us
    pallas_call x1, Pallas kernels, outer(): pl.pallas_call(outer_kernel, out_shape=jax.ShapeDtypeStruct((takers, SUB,...  2.68 us
  transfers between devices with their start and end apart: 4, of which 3 were waited for; matrix products, arithmetic and copies ran while one was open for 0% of the time, Pallas kernels for 8%

profile of v3, /device:TPU:1, one launch (start us, length us, event | category | flops | bytes accessed | tf_op | source)
XLA Modules:
  0.0 54.0 jit_solution(5832154802134413390)
XLA Ops:
  0.0 4.0 %sketch_away.1 = f32[64,512]{1,0:T(8,128)S(1)} custom-call(s32[28]{0:T(128)} %hid_kind.3, s32[28]{0:T(128)} %hid_sign.3, s32[8]{0:T(128)} %out_kind.3, s32[8]{0:T(128)} %out_sign.3, bf16[8,32,128]{2,1,0:T(8,128)(2,1)} %bitcast.2, bf16[8,32,128]{2,1,0:T(8,128)(2,1)} %bitcast.4, bf16[1024,3584]{1,0:T(8,128)(2,1)} %hidden.3, bf16[1024,1024]{1,0:T(8,128)(2,1)} %out_grad.3), custom_call_target="tpu_custom_call" | custom-call | tf_op jit(solution)/shard_map/sketch_away/pallas_call | solution.py:85
  4.1 2.6 %collective-permute-start = (f32[64,512]{1,0:T(8,128)S(1)}, f32[64,512]{1,0:T(8,128)S(1)}, u32[]{:S(2)}, u32[]{:S(2)}) collective-permute-start(f32[64,512]{1,0:T(8,128)S(1)} %sketch_away.1), channel_id=1, source_target_pairs={{0,1},{1,0},{2,3},{3,2},{4,5},{5,4},{6,7},{7,6},{8,9},{9,8},{10,11... | collective-permute-start | bytes 393224 | tf_op jit(solution)/shard_map/ppermute | solution.py:298
  6.6 4.1 %sketch_own.1 = f32[64,512]{1,0:T(8,128)S(1)} custom-call(s32[28]{0:T(128)} %hid_kind.3, s32[28]{0:T(128)} %hid_sign.3, s32[8]{0:T(128)} %out_kind.3, s32[8]{0:T(128)} %out_sign.3, bf16[8,32,128]{2,1,0:T(8,128)(2,1)} %bitcast.3, bf16[8,32,128]{2,1,0:T(8,128)(2,1)} %bitcast.5, bf16[1024,3584]{1,0:T(8,128)(2,1)} %hidden.3, bf16[1024,1024]{1,0:T(8,128)(2,1)} %out_grad.3), custom_call_target="tpu_custom_call" | custom-call | tf_op jit(solution)/shard_map/sketch_own/pallas_call | solution.py:85
  10.7 0.0 collective-permute-done
  10.7 4.8 %collective-permute-start.1 = (f32[64,512]{1,0:T(8,128)S(1)}, f32[64,512]{1,0:T(8,128)S(1)}, u32[]{:S(2)}, u32[]{:S(2)}) collective-permute-start(f32[64,512]{1,0:T(8,128)S(1)} %add.6), channel_id=1, source_target_pairs={{0,7},{1,2},{2,1},{3,4},{4,3},{5,6},{6,5},{7,0},{8,15},{9,10},{10,... | collective-permute-start | bytes 393224 | tf_op jit(solution)/shard_map/ppermute | solution.py:298
  15.5 2.8 %collective-permute-done.1 = f32[64,512]{1,0:T(8,128)S(1)} collective-permute-done((f32[64,512]{1,0:T(8,128)S(1)}, f32[64,512]{1,0:T(8,128)S(1)}, u32[]{:S(2)}, u32[]{:S(2)}) %collective-permute-start.1) | collective-permute-done | bytes 131104 | tf_op jit(solution)/shard_map/ppermute | solution.py:298
  18.3 0.0 copy-start
  18.3 1.3 %collective-permute-start.2 = (f32[64,512]{1,0:T(8,128)S(1)}, f32[64,512]{1,0:T(8,128)S(1)}, u32[]{:S(2)}, u32[]{:S(2)}) collective-permute-start(f32[64,512]{1,0:T(8,128)S(1)} %add.7.x_ref), channel_id=1, source_target_pairs={{0,3},{1,6},{2,5},{3,0},{4,7},{5,2},{6,1},{7,4},{8,11},{9,14},{10,... | collective-permute-start | bytes 393224 | tf_op jit(solution)/shard_map/ppermute | solution.py:298
  19.6 7.2 %collective-permute-done.2.other = f32[64,512]{1,0:T(8,128)S(1)} collective-permute-done((f32[64,512]{1,0:T(8,128)S(1)}, f32[64,512]{1,0:T(8,128)S(1)}, u32[]{:S(2)}, u32[]{:S(2)}) %collective-permute-start.2) | collective-permute-done | bytes 131104 | tf_op jit(solution)/shard_map/ppermute | solution.py:298
  26.8 0.0 copy-done
  26.8 0.0 copy-start.1
  26.8 0.6 %copy-done.1 = f32[64,512]{1,0:T(8,128)} copy-done((f32[64,512]{1,0:T(8,128)}, f32[64,512]{1,0:T(8,128)S(1)}, u32[]{:S(2)}) %copy-start.1) | copy-done | bytes 131096
  27.5 2.7 %outer.1 = f32[64,8,128]{2,1,0:T(8,128)} custom-call(s32[2]{0:T(128)} %lengths.1, f32[64,512]{1,0:T(8,128)} %copy-done, f32[64,512]{1,0:T(8,128)} %copy-done.1), custom_call_target="tpu_custom_call" | custom-call | tf_op jit(solution)/shard_map/outer/pallas_call | solution.py:143
  30.1 9.4 %all-to-all-start = ((f32[64,8,128]{2,1,0:T(8,128)}), f32[64,8,128]{2,1,0:T(8,128)S(1)}, u32[]{:S(2)}, u32[]{:S(2)}) async-start(f32[64,8,128]{2,1,0:T(8,128)} %outer.1), calls=%async_computation | async-start | bytes 524288 | tf_op jit(solution)/shard_map/all_to_all | solution.py:305
  40.3 9.0 %all-to-all-done.gathered = f32[64,8,128]{2,1,0:T(8,128)S(1)} async-done(((f32[64,8,128]{2,1,0:T(8,128)}), f32[64,8,128]{2,1,0:T(8,128)S(1)}, u32[]{:S(2)}, u32[]{:S(2)}) %all-to-all-start) | async-done | bytes 262176 | tf_op jit(solution)/shard_map/all_to_all | solution.py:305
  49.2 4.8 %whiten.1 = f32[2,1024]{1,0:T(2,128)} custom-call(f32[1]{0:T(128)S(6)} %copy.11.ridge, f32[64,8,128]{2,1,0:T(8,128)S(1)} %all-to-all-done.gathered), custom_call_target="tpu_custom_call" | custom-call | tf_op jit(solution)/shard_map/whiten/pallas_call | solution.py:268
  (2 shorter events, 0.0 us)
Async XLA Ops:
  4.1 6.6 %collective-permute-start = (f32[64,512]{1,0:T(8,128)S(1)}, f32[64,512]{1,0:T(8,128)S(1)}, u32[]{:S(2)}, u32[]{:S(2)}) collective-permute-start(f32[64,512]{1,0:T(8,128)S(1)} %sketch_away.1), channel_id=1, source_target_pairs={{0,1},{1,0},{2,3},{3,2},{4,5},{5,4},{6,7},{7,6},{8,9},{9,8},{10,11... | collective-permute-start | bytes 393224 | tf_op jit(solution)/shard_map/ppermute | solution.py:298
  10.7 7.5 %collective-permute-start.1 = (f32[64,512]{1,0:T(8,128)S(1)}, f32[64,512]{1,0:T(8,128)S(1)}, u32[]{:S(2)}, u32[]{:S(2)}) collective-permute-start(f32[64,512]{1,0:T(8,128)S(1)} %add.6), channel_id=1, source_target_pairs={{0,7},{1,2},{2,1},{3,4},{4,3},{5,6},{6,5},{7,0},{8,15},{9,10},{10,... | collective-permute-start | bytes 393224 | tf_op jit(solution)/shard_map/ppermute | solution.py:298
  18.3 8.6 %copy-start = (f32[64,512]{1,0:T(8,128)}, f32[64,512]{1,0:T(8,128)S(1)}, u32[]{:S(2)}) copy-start(f32[64,512]{1,0:T(8,128)S(1)} %add.7.x_ref) | copy-start | bytes 393220
  18.3 8.5 %collective-permute-start.2 = (f32[64,512]{1,0:T(8,128)S(1)}, f32[64,512]{1,0:T(8,128)S(1)}, u32[]{:S(2)}, u32[]{:S(2)}) collective-permute-start(f32[64,512]{1,0:T(8,128)S(1)} %add.7.x_ref), channel_id=1, source_target_pairs={{0,3},{1,6},{2,5},{3,0},{4,7},{5,2},{6,1},{7,4},{8,11},{9,14},{10,... | collective-permute-start | bytes 393224 | tf_op jit(solution)/shard_map/ppermute | solution.py:298
  26.8 0.7 %copy-start.1 = (f32[64,512]{1,0:T(8,128)}, f32[64,512]{1,0:T(8,128)S(1)}, u32[]{:S(2)}) copy-start(f32[64,512]{1,0:T(8,128)S(1)} %collective-permute-done.2.other) | copy-start | bytes 393220
  30.1 19.1 %all-to-all-start = ((f32[64,8,128]{2,1,0:T(8,128)}), f32[64,8,128]{2,1,0:T(8,128)S(1)}, u32[]{:S(2)}, u32[]{:S(2)}) async-start(f32[64,8,128]{2,1,0:T(8,128)} %outer.1), calls=%async_computation | async-start | bytes 524288 | tf_op jit(solution)/shard_map/all_to_all | solution.py:305

commit v4 on v3

--- a/solution.py
+++ b/solution.py
@@ -25,8 +25,8 @@
 
 
 def sketch_kernel(
-    away, hid_kind, hid_sign, out_kind, out_sign, hid_table, out_table, hidden, out_grad, x,
-    hid_buf, out_buf, hid_tab, out_tab, hid_pick, hid_neg, out_pick, out_neg, s_in, s_out, small_sems, hid_sems, out_sem,
+    away, lengths, hid_kind, hid_sign, out_kind, out_sign, hid_table, out_table, hidden, out_grad, x,
+    hid_buf, out_buf, hid_tab, out_tab, counts, hid_pick, hid_neg, out_pick, out_neg, s_in, s_out, small_sems, hid_sems, out_sem,
 ):
     which = kept(lax.axis_index("tensor"))
     which = 1 - which if away else which
@@ -41,6 +41,7 @@
                 (hid_sign, hid_neg),
                 (out_table, out_tab),
                 (hid_table, hid_tab),
+                (lengths, counts),
             ]
         )
     ]
@@ -76,35 +77,40 @@
         hid_copies[c].wait()
         part = times(s_in[:, c * depth : (c + 1) * depth], hid_buf[c])
         total = part if total is None else total + part
-    x[:width, :] = total
-
-
-def sketch(away, hidden, out_grad, hid_kind, hid_sign, hid_table, out_kind, out_sign, out_table, length):
+    count = counts[which]
+    live = iota(total.shape, 1) < count
+    scale = lax.rsqrt(jnp.full((1, total.shape[1]), count, jnp.int32).astype(F32))
+    x[:width, :] = jnp.where(live, total * scale, 0.0)
+
+
+def sketch(away, hidden, out_grad, lengths, hid_kind, hid_sign, hid_table, out_kind, out_sign, out_table, length):
     deep, wide = hidden.shape[1], out_grad.shape[1]
     chunks = 7
+    operands = (lengths, hid_kind, hid_sign, out_kind, out_sign, hid_table, out_table, hidden, out_grad)
     return pl.pallas_call(
         functools.partial(sketch_kernel, away),
         out_shape=jax.ShapeDtypeStruct((2 * hid_table.shape[1], length), F32),
-        in_specs=[HBM] * 8,
+        in_specs=[HBM] * len(operands),
         out_specs=VMEM,
         scratch_shapes=[
             pltpu.VMEM((chunks, length, deep // chunks), BF16),
             pltpu.VMEM((length, wide), BF16),
             pltpu.VMEM(hid_table.shape, BF16),
             pltpu.VMEM(out_table.shape, BF16),
+            pltpu.SMEM(lengths.shape, jnp.int32),
             pltpu.SMEM(hid_kind.shape, jnp.int32),
             pltpu.SMEM(hid_sign.shape, jnp.int32),
             pltpu.SMEM(out_kind.shape, jnp.int32),
             pltpu.SMEM(out_sign.shape, jnp.int32),
             pltpu.VMEM((hid_table.shape[1], deep), BF16),
             pltpu.VMEM((out_table.shape[1], wide), BF16),
-            pltpu.SemaphoreType.DMA((6,)),
+            pltpu.SemaphoreType.DMA((7,)),
             pltpu.SemaphoreType.DMA((chunks,)),
             pltpu.SemaphoreType.DMA,
         ],
         compiler_params=pltpu.CompilerParams(vmem_limit_bytes=24 * 2**20),
         name="sketch_away" if away else "sketch_own",
-    )(*[pltpu.with_memory_space_constraint(v, pltpu.HBM) for v in (hid_kind, hid_sign, out_kind, out_sign, hid_table, out_table, hidden, out_grad)])
+    )(*[pltpu.with_memory_space_constraint(v, pltpu.HBM) for v in operands])
 
 
 def split(x, parts):
@@ -116,38 +122,33 @@
     return out
 
 
-def outer_kernel(lengths, x_ref, other, feats, counts, sem):
-    copy = pltpu.make_async_copy(lengths, counts, sem)
-    copy.start()
+def outer_kernel(x_ref, other, feats):
     x = x_ref[...] + other[...]
     width = x.shape[0] // 2
-    copy.wait()
-    count = counts[kept(lax.axis_index("tensor"))]
-    a = jnp.where(iota((width, x.shape[1]), 1) < count, x[:width], 0.0)
-    a = jnp.concatenate(split(a, 2), axis=0)
+    a = jnp.concatenate(split(x[:width], 2), axis=0)
     b = jnp.concatenate(split(x[width:], 2), axis=0)
     z = lax.dot_general(b, a, (((1,), (1,)), ((), ())), preferred_element_type=F32)
     z = z[:width] + z[width:]
     spread = (iota((2 * width, LANES), 0) % width == iota((2 * width, LANES), 1) // 4).astype(BF16)
-    y = sum(jnp.dot(piece, spread, preferred_element_type=F32) for piece in split(z, 3))
+    y = jnp.dot(jnp.concatenate(split(z, 3), axis=0), spread, preferred_element_type=F32)
+    y = y[:width] + y[width : 2 * width] + y[2 * width :]
     own = iota((SUB, LANES), 1) % 4
     total = jnp.zeros((SUB, LANES), F32)
     for q in range(4):
         total += jnp.where(own == q, y[q * SUB : (q + 1) * SUB], 0.0)
-    total *= lax.rsqrt(jnp.full((SUB, LANES), count, jnp.int32).astype(F32))
     for n in range(feats.shape[0]):
         feats[n] = total
 
 
-def outer(lengths, x, other, takers):
+def outer(x, other, takers):
     return pl.pallas_call(
         outer_kernel,
         out_shape=jax.ShapeDtypeStruct((takers, SUB, LANES), F32),
-        in_specs=[HBM, VMEM, VMEM],
+        in_specs=[VMEM, VMEM],
         out_specs=VMEM,
-        scratch_shapes=[pltpu.SMEM(lengths.shape, jnp.int32), pltpu.SemaphoreType.DMA],
+        compiler_params=pltpu.CompilerParams(vmem_limit_bytes=8 * 2**20),
         name="outer",
-    )(lengths, x, other)
+    )(x, other)
 
 
 def whiten_kernel(ridge, gathered, out, aug, across, prods, ridge_here, sem):
@@ -290,7 +291,7 @@
 
     def of(away):
         return sketch(
-            away, hidden, out_grad, hid_kind, hid_sign, hid_table.swapaxes(1, 2),
+            away, hidden, out_grad, lengths, hid_kind, hid_sign, hid_table.swapaxes(1, 2),
             out_kind, out_sign, out_table.swapaxes(1, 2), length,
         )
 
@@ -300,7 +301,7 @@
     x = of(True)
     x = of(False) + swap(x, lambda i: i ^ 1)
     x = x + swap(x, lambda i: i + 1 if i % 2 else i - 1)
-    feats = outer(lengths, x, swap(x, lambda i: i - 3 if i % 2 else i + 3), 2 * dp)
+    feats = outer(x, swap(x, lambda i: i - 3 if i % 2 else i + 3), 2 * dp)
     groups = [[d * tensor + z + h for d in range(dp) for h in range(2)] for z in range(0, tensor, 2)]
     gathered = lax.all_to_all(feats, ("dp", "tensor"), 0, 0, axis_index_groups=groups)
     return whiten(ridge, gathered)

time: 54.2 us -> 52 us (0.959)
  Pallas kernels: 15.6 us -> 14 us
  local copies, waits for them, and re-layouts: 0.65 us -> 0 us
    pallas_call x1, Pallas kernels: 2.68 us -> 1.01 us  [outer(): pl.pallas_call(outer_kernel, out_shape=jax.ShapeDtypeStruct((takers, SUB,...]
    unnamed x4 -> x0, local copies, waits for them, and re-layouts: 0.65 us -> none
where the time goes in v4:
time: 52 us; the launch traced here: 51.8 us
  waiting for transfers between devices  19 us (37%)
  starting transfers between devices  18.1 us (35%)
  Pallas kernels  14 us (27%)
  between operations  0.69 us (1%)
    ppermute x3, waiting for transfers between devices, swap(): lax.ppermute(x, 'tensor', [(i, other(i) % tensor) for i in range(tensor)])  10 us
    all_to_all x1, starting transfers between devices, per_device(): lax.all_to_all(feats, ('dp', 'tensor'), 0, 0, axis_index_groups=groups)  9.54 us
    all_to_all x1, waiting for transfers between devices, per_device(): lax.all_to_all(feats, ('dp', 'tensor'), 0, 0, axis_index_groups=groups)  8.97 us
    ppermute x3, starting transfers between devices, swap(): lax.ppermute(x, 'tensor', [(i, other(i) % tensor) for i in range(tensor)])  8.61 us
    pallas_call x2, Pallas kernels, sketch(): pl.pallas_call(functools.partial(sketch_kernel, away), out_shape=jax.Shap...  8.16 us
    pallas_call x1, Pallas kernels, whiten(): pl.pallas_call(whiten_kernel, out_shape=jax.ShapeDtypeStruct((2, SUB * LA...  4.82 us
  transfers between devices with their start and end apart: 4, of which 3 were waited for; matrix products, arithmetic and copies ran while one was open for 0% of the time, Pallas kernels for 8%

profile of v4, /device:TPU:1, one launch (start us, length us, event | category | flops | bytes accessed | tf_op | source)
XLA Modules:
  0.0 51.8 jit_solution(11646943441722501229)
XLA Ops:
  0.0 4.1 %sketch_away.1 = f32[64,512]{1,0:T(8,128)S(1)} custom-call(s32[2]{0:T(128)} %lengths.3, s32[28]{0:T(128)} %hid_kind.3, s32[28]{0:T(128)} %hid_sign.3, s32[8]{0:T(128)} %out_kind.3, s32[8]{0:T(128)} %out_sign.3, bf16[8,32,128]{2,1,0:T(8,128)(2,1)} %bitcast.2, bf16[8,32,128]{2,1,0:T(8,128)(2,1)} %bitcast.4, bf16[1024,3584]{1,0:T(8,128)(2,1)} %hidden.3, ...), custom_call_target="tpu_custom_call" | custom-call | tf_op jit(solution)/shard_map/sketch_away/pallas_call | solution.py:90
  4.1 2.6 %collective-permute-start = (f32[64,512]{1,0:T(8,128)S(1)}, f32[64,512]{1,0:T(8,128)S(1)}, u32[]{:S(2)}, u32[]{:S(2)}) collective-permute-start(f32[64,512]{1,0:T(8,128)S(1)} %sketch_away.1), channel_id=1, source_target_pairs={{0,1},{1,0},{2,3},{3,2},{4,5},{5,4},{6,7},{7,6},{8,9},{9,8},{10,11... | collective-permute-start | bytes 393224 | tf_op jit(solution)/shard_map/ppermute | solution.py:299
  6.6 4.1 %sketch_own.1 = f32[64,512]{1,0:T(8,128)S(1)} custom-call(s32[2]{0:T(128)} %lengths.3, s32[28]{0:T(128)} %hid_kind.3, s32[28]{0:T(128)} %hid_sign.3, s32[8]{0:T(128)} %out_kind.3, s32[8]{0:T(128)} %out_sign.3, bf16[8,32,128]{2,1,0:T(8,128)(2,1)} %bitcast.3, bf16[8,32,128]{2,1,0:T(8,128)(2,1)} %bitcast.5, bf16[1024,3584]{1,0:T(8,128)(2,1)} %hidden.3, ...), custom_call_target="tpu_custom_call" | custom-call | tf_op jit(solution)/shard_map/sketch_own/pallas_call | solution.py:90
  10.7 0.0 collective-permute-done
  10.8 4.8 %collective-permute-start.1 = (f32[64,512]{1,0:T(8,128)S(1)}, f32[64,512]{1,0:T(8,128)S(1)}, u32[]{:S(2)}, u32[]{:S(2)}) collective-permute-start(f32[64,512]{1,0:T(8,128)S(1)} %add.6), channel_id=1, source_target_pairs={{0,7},{1,2},{2,1},{3,4},{4,3},{5,6},{6,5},{7,0},{8,15},{9,10},{10,... | collective-permute-start | bytes 393224 | tf_op jit(solution)/shard_map/ppermute | solution.py:299
  15.5 2.8 %collective-permute-done.1 = f32[64,512]{1,0:T(8,128)S(1)} collective-permute-done((f32[64,512]{1,0:T(8,128)S(1)}, f32[64,512]{1,0:T(8,128)S(1)}, u32[]{:S(2)}, u32[]{:S(2)}) %collective-permute-start.1) | collective-permute-done | bytes 131104 | tf_op jit(solution)/shard_map/ppermute | solution.py:299
  18.3 1.3 %collective-permute-start.2 = (f32[64,512]{1,0:T(8,128)S(1)}, f32[64,512]{1,0:T(8,128)S(1)}, u32[]{:S(2)}, u32[]{:S(2)}) collective-permute-start(f32[64,512]{1,0:T(8,128)S(1)} %add.7.x_ref), channel_id=1, source_target_pairs={{0,3},{1,6},{2,5},{3,0},{4,7},{5,2},{6,1},{7,4},{8,11},{9,14},{10,... | collective-permute-start | bytes 393224 | tf_op jit(solution)/shard_map/ppermute | solution.py:299
  19.6 7.2 %collective-permute-done.2.other = f32[64,512]{1,0:T(8,128)S(1)} collective-permute-done((f32[64,512]{1,0:T(8,128)S(1)}, f32[64,512]{1,0:T(8,128)S(1)}, u32[]{:S(2)}, u32[]{:S(2)}) %collective-permute-start.2) | collective-permute-done | bytes 131104 | tf_op jit(solution)/shard_map/ppermute | solution.py:299
  26.9 1.0 %outer.1 = f32[64,8,128]{2,1,0:T(8,128)} custom-call(f32[64,512]{1,0:T(8,128)S(1)} %add.7.x_ref, f32[64,512]{1,0:T(8,128)S(1)} %collective-permute-done.2.other), custom_call_target="tpu_custom_call" | custom-call | tf_op jit(solution)/shard_map/outer/pallas_call | solution.py:144
  27.9 9.5 %all-to-all-start = ((f32[64,8,128]{2,1,0:T(8,128)}), f32[64,8,128]{2,1,0:T(8,128)S(1)}, u32[]{:S(2)}, u32[]{:S(2)}) async-start(f32[64,8,128]{2,1,0:T(8,128)} %outer.1), calls=%async_computation | async-start | bytes 524288 | tf_op jit(solution)/shard_map/all_to_all | solution.py:306
  38.1 9.0 %all-to-all-done.gathered = f32[64,8,128]{2,1,0:T(8,128)S(1)} async-done(((f32[64,8,128]{2,1,0:T(8,128)}), f32[64,8,128]{2,1,0:T(8,128)S(1)}, u32[]{:S(2)}, u32[]{:S(2)}) %all-to-all-start) | async-done | bytes 262176 | tf_op jit(solution)/shard_map/all_to_all | solution.py:306
  47.0 4.8 %whiten.1 = f32[2,1024]{1,0:T(2,128)} custom-call(f32[1]{0:T(128)S(6)} %copy.11.ridge, f32[64,8,128]{2,1,0:T(8,128)S(1)} %all-to-all-done.gathered), custom_call_target="tpu_custom_call" | custom-call | tf_op jit(solution)/shard_map/whiten/pallas_call | solution.py:269
  (2 shorter events, 0.0 us)
Async XLA Ops:
  4.1 6.6 %collective-permute-start = (f32[64,512]{1,0:T(8,128)S(1)}, f32[64,512]{1,0:T(8,128)S(1)}, u32[]{:S(2)}, u32[]{:S(2)}) collective-permute-start(f32[64,512]{1,0:T(8,128)S(1)} %sketch_away.1), channel_id=1, source_target_pairs={{0,1},{1,0},{2,3},{3,2},{4,5},{5,4},{6,7},{7,6},{8,9},{9,8},{10,11... | collective-permute-start | bytes 393224 | tf_op jit(solution)/shard_map/ppermute | solution.py:299
  10.8 7.5 %collective-permute-start.1 = (f32[64,512]{1,0:T(8,128)S(1)}, f32[64,512]{1,0:T(8,128)S(1)}, u32[]{:S(2)}, u32[]{:S(2)}) collective-permute-start(f32[64,512]{1,0:T(8,128)S(1)} %add.6), channel_id=1, source_target_pairs={{0,7},{1,2},{2,1},{3,4},{4,3},{5,6},{6,5},{7,0},{8,15},{9,10},{10,... | collective-permute-start | bytes 393224 | tf_op jit(solution)/shard_map/ppermute | solution.py:299
  18.3 8.5 %collective-permute-start.2 = (f32[64,512]{1,0:T(8,128)S(1)}, f32[64,512]{1,0:T(8,128)S(1)}, u32[]{:S(2)}, u32[]{:S(2)}) collective-permute-start(f32[64,512]{1,0:T(8,128)S(1)} %add.7.x_ref), channel_id=1, source_target_pairs={{0,3},{1,6},{2,5},{3,0},{4,7},{5,2},{6,1},{7,4},{8,11},{9,14},{10,... | collective-permute-start | bytes 393224 | tf_op jit(solution)/shard_map/ppermute | solution.py:299
  27.9 19.2 %all-to-all-start = ((f32[64,8,128]{2,1,0:T(8,128)}), f32[64,8,128]{2,1,0:T(8,128)S(1)}, u32[]{:S(2)}, u32[]{:S(2)}) async-start(f32[64,8,128]{2,1,0:T(8,128)} %outer.1), calls=%async_computation | async-start | bytes 524288 | tf_op jit(solution)/shard_map/all_to_all | solution.py:306

commit v5 on v4

--- a/solution.py
+++ b/solution.py
@@ -26,11 +26,11 @@
 
 def sketch_kernel(
     away, lengths, hid_kind, hid_sign, out_kind, out_sign, hid_table, out_table, hidden, out_grad, x,
-    hid_buf, out_buf, hid_tab, out_tab, counts, hid_pick, hid_neg, out_pick, out_neg, s_in, s_out, small_sems, hid_sems, out_sem,
+    hid_buf, out_buf, hid_tab, out_tab, counts, hid_pick, hid_neg, out_pick, out_neg, s_in, s_out, small_sems, hid_sem, out_sem,
 ):
     which = kept(lax.axis_index("tensor"))
     which = 1 - which if away else which
-    chunks, rows, depth = hid_buf.shape
+    rows, _ = hid_buf.shape
     small = [
         pltpu.make_async_copy(src, dst, small_sems.at[n])
         for n, (src, dst) in enumerate(
@@ -50,12 +50,8 @@
     here = pl.ds(pl.multiple_of(which * rows, rows), rows)
     out_copy = pltpu.make_async_copy(out_grad.at[here], out_buf, out_sem)
     out_copy.start()
-    hid_copies = [
-        pltpu.make_async_copy(hidden.at[here, pl.ds(c * depth, depth)], hid_buf.at[c], hid_sems.at[c])
-        for c in range(chunks)
-    ]
-    for copy in hid_copies:
-        copy.start()
+    hid_copy = pltpu.make_async_copy(hidden.at[here], hid_buf, hid_sem)
+    hid_copy.start()
     _, width, size = hid_tab.shape
     for copy in small:
         copy.wait()
@@ -72,11 +68,8 @@
     fill(hid_pick, hid_neg, hid_tab, s_in)
     out_copy.wait()
     x[width:, :] = times(s_out[...], out_buf[...])
-    total = None
-    for c in range(chunks):
-        hid_copies[c].wait()
-        part = times(s_in[:, c * depth : (c + 1) * depth], hid_buf[c])
-        total = part if total is None else total + part
+    hid_copy.wait()
+    total = times(s_in[...], hid_buf[...])
     count = counts[which]
     live = iota(total.shape, 1) < count
     scale = lax.rsqrt(jnp.full((1, total.shape[1]), count, jnp.int32).astype(F32))
@@ -85,7 +78,6 @@
 
 def sketch(away, hidden, out_grad, lengths, hid_kind, hid_sign, hid_table, out_kind, out_sign, out_table, length):
     deep, wide = hidden.shape[1], out_grad.shape[1]
-    chunks = 7
     operands = (lengths, hid_kind, hid_sign, out_kind, out_sign, hid_table, out_table, hidden, out_grad)
     return pl.pallas_call(
         functools.partial(sketch_kernel, away),
@@ -93,7 +85,7 @@
         in_specs=[HBM] * len(operands),
         out_specs=VMEM,
         scratch_shapes=[
-            pltpu.VMEM((chunks, length, deep // chunks), BF16),
+            pltpu.VMEM((length, deep), BF16),
             pltpu.VMEM((length, wide), BF16),
             pltpu.VMEM(hid_table.shape, BF16),
             pltpu.VMEM(out_table.shape, BF16),
@@ -105,7 +97,7 @@
             pltpu.VMEM((hid_table.shape[1], deep), BF16),
             pltpu.VMEM((out_table.shape[1], wide), BF16),
             pltpu.SemaphoreType.DMA((7,)),
-            pltpu.SemaphoreType.DMA((chunks,)),
+            pltpu.SemaphoreType.DMA,
             pltpu.SemaphoreType.DMA,
         ],
         compiler_params=pltpu.CompilerParams(vmem_limit_bytes=24 * 2**20),
@@ -186,7 +178,7 @@
     for i8 in range(groups):
         wide = seqs - i8 * SUB
         block = prods[i8 * SUB : (i8 + 1) * SUB, i8 * SUB : seqs, :].reshape(SUB * wide, LANES)
-        total = sum(jnp.dot(piece, before, preferred_element_type=F32) for piece in split(block, 3))
+        total = sum(jnp.dot(piece, before, preferred_element_type=F32) for piece in split(block, 2))
         aug[i8 * SUB : (i8 + 1) * SUB, i8 * SUB : seqs, :] = total.reshape(SUB, wide, LANES)
     copy.wait()
     r = ridge_here[0]

time: 52 us -> 50.2 us (0.965)
  waiting for transfers between devices: 19 us -> 16.7 us
  starting transfers between devices: 18.1 us -> 19.5 us
  Pallas kernels: 14 us -> 13 us
    ppermute x3, waiting for transfers between devices: 10 us -> 7.76 us  [swap(): lax.ppermute(x, 'tensor', [(i, other(i) % tensor) for i in range(tensor)])]
    all_to_all x1, starting transfers between devices: 9.54 us -> 10.5 us  [per_device(): lax.all_to_all(feats, ('dp', 'tensor'), 0, 0, axis_index_groups=groups)]
    pallas_call x2, Pallas kernels: 8.16 us -> 7.37 us  [sketch(): pl.pallas_call(functools.partial(sketch_kernel, away), out_shape=jax.Shap...]
  transfers between devices with their start and end apart: 4 -> 4, of which waited for: 3 -> 3; matrix products, arithmetic and copies ran while one was open for 0% -> 0% of each run, Pallas kernels for 8% -> 7%
where the time goes in v5:
time: 50.2 us; the launch traced here: 50 us
  starting transfers between devices  19.5 us (39%)
  waiting for transfers between devices  16.7 us (33%)
  Pallas kernels  13 us (26%)
  between operations  0.69 us (1%)
    all_to_all x1, starting transfers between devices, per_device(): lax.all_to_all(feats, ('dp', 'tensor'), 0, 0, axis_index_groups=groups)  10.5 us
    ppermute x3, starting transfers between devices, swap(): lax.ppermute(x, 'tensor', [(i, other(i) % tensor) for i in range(tensor)])  9.02 us
    all_to_all x1, waiting for transfers between devices, per_device(): lax.all_to_all(feats, ('dp', 'tensor'), 0, 0, axis_index_groups=groups)  8.97 us
    ppermute x3, waiting for transfers between devices, swap(): lax.ppermute(x, 'tensor', [(i, other(i) % tensor) for i in range(tensor)])  7.76 us
    pallas_call x2, Pallas kernels, sketch(): pl.pallas_call(functools.partial(sketch_kernel, away), out_shape=jax.Shap...  7.37 us
    pallas_call x1, Pallas kernels, whiten(): pl.pallas_call(whiten_kernel, out_shape=jax.ShapeDtypeStruct((2, SUB * LA...  4.64 us
    pallas_call x1, Pallas kernels, outer(): pl.pallas_call(outer_kernel, out_shape=jax.ShapeDtypeStruct((takers, SUB,...  1.01 us
  transfers between devices with their start and end apart: 4, of which 3 were waited for; matrix products, arithmetic and copies ran while one was open for 0% of the time, Pallas kernels for 7%

profile of v5, /device:TPU:1, one launch (start us, length us, event | category | flops | bytes accessed | tf_op | source)
XLA Modules:
  0.0 50.0 jit_solution(6731681505637885154)
XLA Ops:
  0.0 3.7 %sketch_away.1 = f32[64,512]{1,0:T(8,128)S(1)} custom-call(s32[2]{0:T(128)} %lengths.3, s32[28]{0:T(128)} %hid_kind.3, s32[28]{0:T(128)} %hid_sign.3, s32[8]{0:T(128)} %out_kind.3, s32[8]{0:T(128)} %out_sign.3, bf16[8,32,128]{2,1,0:T(8,128)(2,1)} %bitcast.2, bf16[8,32,128]{2,1,0:T(8,128)(2,1)} %bitcast.4, bf16[1024,3584]{1,0:T(8,128)(2,1)} %hidden.3, ...), custom_call_target="tpu_custom_call" | custom-call | tf_op jit(solution)/shard_map/sketch_away/pallas_call | solution.py:82
  3.7 2.6 %collective-permute-start = (f32[64,512]{1,0:T(8,128)S(1)}, f32[64,512]{1,0:T(8,128)S(1)}, u32[]{:S(2)}, u32[]{:S(2)}) collective-permute-start(f32[64,512]{1,0:T(8,128)S(1)} %sketch_away.1), channel_id=1, source_target_pairs={{0,1},{1,0},{2,3},{3,2},{4,5},{5,4},{6,7},{7,6},{8,9},{9,8},{10,11... | collective-permute-start | bytes 393224 | tf_op jit(solution)/shard_map/ppermute | solution.py:291
  6.2 3.7 %sketch_own.1 = f32[64,512]{1,0:T(8,128)S(1)} custom-call(s32[2]{0:T(128)} %lengths.3, s32[28]{0:T(128)} %hid_kind.3, s32[28]{0:T(128)} %hid_sign.3, s32[8]{0:T(128)} %out_kind.3, s32[8]{0:T(128)} %out_sign.3, bf16[8,32,128]{2,1,0:T(8,128)(2,1)} %bitcast.3, bf16[8,32,128]{2,1,0:T(8,128)(2,1)} %bitcast.5, bf16[1024,3584]{1,0:T(8,128)(2,1)} %hidden.3, ...), custom_call_target="tpu_custom_call" | custom-call | tf_op jit(solution)/shard_map/sketch_own/pallas_call | solution.py:82
  9.9 0.0 collective-permute-done
  10.0 4.8 %collective-permute-start.1 = (f32[64,512]{1,0:T(8,128)S(1)}, f32[64,512]{1,0:T(8,128)S(1)}, u32[]{:S(2)}, u32[]{:S(2)}) collective-permute-start(f32[64,512]{1,0:T(8,128)S(1)} %add.6), channel_id=1, source_target_pairs={{0,7},{1,2},{2,1},{3,4},{4,3},{5,6},{6,5},{7,0},{8,15},{9,10},{10,... | collective-permute-start | bytes 393224 | tf_op jit(solution)/shard_map/ppermute | solution.py:291
  14.7 2.4 %collective-permute-done.1 = f32[64,512]{1,0:T(8,128)S(1)} collective-permute-done((f32[64,512]{1,0:T(8,128)S(1)}, f32[64,512]{1,0:T(8,128)S(1)}, u32[]{:S(2)}, u32[]{:S(2)}) %collective-permute-start.1) | collective-permute-done | bytes 131104 | tf_op jit(solution)/shard_map/ppermute | solution.py:291
  17.1 1.7 %collective-permute-start.2 = (f32[64,512]{1,0:T(8,128)S(1)}, f32[64,512]{1,0:T(8,128)S(1)}, u32[]{:S(2)}, u32[]{:S(2)}) collective-permute-start(f32[64,512]{1,0:T(8,128)S(1)} %add.7.x_ref), channel_id=1, source_target_pairs={{0,3},{1,6},{2,5},{3,0},{4,7},{5,2},{6,1},{7,4},{8,11},{9,14},{10,... | collective-permute-start | bytes 393224 | tf_op jit(solution)/shard_map/ppermute | solution.py:291
  18.8 5.4 %collective-permute-done.2.other = f32[64,512]{1,0:T(8,128)S(1)} collective-permute-done((f32[64,512]{1,0:T(8,128)S(1)}, f32[64,512]{1,0:T(8,128)S(1)}, u32[]{:S(2)}, u32[]{:S(2)}) %collective-permute-start.2) | collective-permute-done | bytes 131104 | tf_op jit(solution)/shard_map/ppermute | solution.py:291
  24.2 1.0 %outer.1 = f32[64,8,128]{2,1,0:T(8,128)} custom-call(f32[64,512]{1,0:T(8,128)S(1)} %add.7.x_ref, f32[64,512]{1,0:T(8,128)S(1)} %collective-permute-done.2.other), custom_call_target="tpu_custom_call" | custom-call | tf_op jit(solution)/shard_map/outer/pallas_call | solution.py:136
  25.2 10.5 %all-to-all-start = ((f32[64,8,128]{2,1,0:T(8,128)}), f32[64,8,128]{2,1,0:T(8,128)S(1)}, u32[]{:S(2)}, u32[]{:S(2)}) async-start(f32[64,8,128]{2,1,0:T(8,128)} %outer.1), calls=%async_computation | async-start | bytes 524288 | tf_op jit(solution)/shard_map/all_to_all | solution.py:298
  36.4 9.0 %all-to-all-done.gathered = f32[64,8,128]{2,1,0:T(8,128)S(1)} async-done(((f32[64,8,128]{2,1,0:T(8,128)}), f32[64,8,128]{2,1,0:T(8,128)S(1)}, u32[]{:S(2)}, u32[]{:S(2)}) %all-to-all-start) | async-done | bytes 262176 | tf_op jit(solution)/shard_map/all_to_all | solution.py:298
  45.4 4.6 %whiten.1 = f32[2,1024]{1,0:T(2,128)} custom-call(f32[1]{0:T(128)S(6)} %copy.11.ridge, f32[64,8,128]{2,1,0:T(8,128)S(1)} %all-to-all-done.gathered), custom_call_target="tpu_custom_call" | custom-call | tf_op jit(solution)/shard_map/whiten/pallas_call | solution.py:261
  (2 shorter events, 0.0 us)
Async XLA Ops:
  3.7 6.3 %collective-permute-start = (f32[64,512]{1,0:T(8,128)S(1)}, f32[64,512]{1,0:T(8,128)S(1)}, u32[]{:S(2)}, u32[]{:S(2)}) collective-permute-start(f32[64,512]{1,0:T(8,128)S(1)} %sketch_away.1), channel_id=1, source_target_pairs={{0,1},{1,0},{2,3},{3,2},{4,5},{5,4},{6,7},{7,6},{8,9},{9,8},{10,11... | collective-permute-start | bytes 393224 | tf_op jit(solution)/shard_map/ppermute | solution.py:291
  10.0 7.1 %collective-permute-start.1 = (f32[64,512]{1,0:T(8,128)S(1)}, f32[64,512]{1,0:T(8,128)S(1)}, u32[]{:S(2)}, u32[]{:S(2)}) collective-permute-start(f32[64,512]{1,0:T(8,128)S(1)} %add.6), channel_id=1, source_target_pairs={{0,7},{1,2},{2,1},{3,4},{4,3},{5,6},{6,5},{7,0},{8,15},{9,10},{10,... | collective-permute-start | bytes 393224 | tf_op jit(solution)/shard_map/ppermute | solution.py:291
  17.1 7.1 %collective-permute-start.2 = (f32[64,512]{1,0:T(8,128)S(1)}, f32[64,512]{1,0:T(8,128)S(1)}, u32[]{:S(2)}, u32[]{:S(2)}) collective-permute-start(f32[64,512]{1,0:T(8,128)S(1)} %add.7.x_ref), channel_id=1, source_target_pairs={{0,3},{1,6},{2,5},{3,0},{4,7},{5,2},{6,1},{7,4},{8,11},{9,14},{10,... | collective-permute-start | bytes 393224 | tf_op jit(solution)/shard_map/ppermute | solution.py:291
  25.2 20.2 %all-to-all-start = ((f32[64,8,128]{2,1,0:T(8,128)}), f32[64,8,128]{2,1,0:T(8,128)S(1)}, u32[]{:S(2)}, u32[]{:S(2)}) async-start(f32[64,8,128]{2,1,0:T(8,128)} %outer.1), calls=%async_computation | async-start | bytes 524288 | tf_op jit(solution)/shard_map/all_to_all | solution.py:298

commit v6 on v5

--- a/solution.py
+++ b/solution.py
@@ -188,7 +188,7 @@
             i = i8 * SUB + ii
             aug[i, i8 * SUB : (i8 + 1) * SUB, :] += jnp.where(sub == ii, r, 0.0)
 
-    for p in range(groups):
+    def panel(p):
         base = p * SUB
         diag = [aug[base + k, base : base + SUB, :] for k in range(SUB)]
         inv = []
@@ -208,25 +208,30 @@
             for k in range(SUB):
                 aug[base + k, j8 * SUB : (j8 + 1) * SUB, :] = rows[k]
 
-        for i8 in range(p + 1, groups + 1):
-            for i0 in range(0, SUB, 4):
-                heads = [
-                    [jnp.broadcast_to(aug[base + k, i8 * SUB + ii : i8 * SUB + ii + 1, :], (SUB, LANES)) for k in range(SUB)]
-                    for ii in range(i0, i0 + 4)
-                ]
-                for j8 in range(i8, groups + 1):
-                    rows = [aug[base + k, j8 * SUB : (j8 + 1) * SUB, :] for k in range(SUB)]
-                    for ii in range(4):
-                        h = heads[ii]
-                        i = i8 * SUB + i0 + ii
-                        acc = aug[i, j8 * SUB : (j8 + 1) * SUB, :]
-                        if 1:
-                            t = [h[k] * rows[k] for k in range(SUB)]
-                            acc = acc - (((t[0] + t[1]) + (t[2] + t[3])) + ((t[4] + t[5]) + (t[6] + t[7])))
-                        else:
-                            for k in range(SUB):
-                                acc = acc - h[k] * rows[k]
-                        aug[i, j8 * SUB : (j8 + 1) * SUB, :] = acc
+    def trail(p, i8):
+        base = p * SUB
+        for i0 in range(0, SUB, 4):
+            heads = [
+                [jnp.broadcast_to(aug[base + k, i8 * SUB + ii : i8 * SUB + ii + 1, :], (SUB, LANES)) for k in range(SUB)]
+                for ii in range(i0, i0 + 4)
+            ]
+            for j8 in range(i8, groups + 1):
+                rows = [aug[base + k, j8 * SUB : (j8 + 1) * SUB, :] for k in range(SUB)]
+                for ii in range(4):
+                    h = heads[ii]
+                    i = i8 * SUB + i0 + ii
+                    acc = aug[i, j8 * SUB : (j8 + 1) * SUB, :]
+                    t = [h[k] * rows[k] for k in range(SUB)]
+                    acc = acc - (((t[0] + t[1]) + (t[2] + t[3])) + ((t[4] + t[5]) + (t[6] + t[7])))
+                    aug[i, j8 * SUB : (j8 + 1) * SUB, :] = acc
+
+    panel(0)
+    for p in range(groups):
+        trail(p, p + 1)
+        if p + 1 < groups:
+            panel(p + 1)
+        for i8 in range(p + 2, groups + 1):
+            trail(p, i8)
 
     end = seqs - 1
     sol_end = aug[end, seqs : seqs + SUB, :] / aug[end, end : end + 1, :]

time: 50.2 us -> 50.1 us (level)
  no operation moved by 1% of the time
where the time goes in v6:
time: 50.1 us; the launch traced here: 49.9 us
  starting transfers between devices  19.5 us (39%)
  waiting for transfers between devices  16.7 us (33%)
  Pallas kernels  12.9 us (26%)
  between operations  0.69 us (1%)
    all_to_all x1, starting transfers between devices, per_device(): lax.all_to_all(feats, ('dp', 'tensor'), 0, 0, axis_index_groups=groups)  10.5 us
    ppermute x3, starting transfers between devices, swap(): lax.ppermute(x, 'tensor', [(i, other(i) % tensor) for i in range(tensor)])  9.02 us
    all_to_all x1, waiting for transfers between devices, per_device(): lax.all_to_all(feats, ('dp', 'tensor'), 0, 0, axis_index_groups=groups)  8.97 us
    ppermute x3, waiting for transfers between devices, swap(): lax.ppermute(x, 'tensor', [(i, other(i) % tensor) for i in range(tensor)])  7.76 us
    pallas_call x2, Pallas kernels, sketch(): pl.pallas_call(functools.partial(sketch_kernel, away), out_shape=jax.Shap...  7.37 us
    pallas_call x1, Pallas kernels, whiten(): pl.pallas_call(whiten_kernel, out_shape=jax.ShapeDtypeStruct((2, SUB * LA...  4.5 us
    pallas_call x1, Pallas kernels, outer(): pl.pallas_call(outer_kernel, out_shape=jax.ShapeDtypeStruct((takers, SUB,...  1.01 us
  transfers between devices with their start and end apart: 4, of which 3 were waited for; matrix products, arithmetic and copies ran while one was open for 0% of the time, Pallas kernels for 7%

profile of v6, /device:TPU:1, one launch (start us, length us, event | category | flops | bytes accessed | tf_op | source)
XLA Modules:
  0.0 49.9 jit_solution(2087800229571885073)
XLA Ops:
  0.0 3.7 %sketch_away.1 = f32[64,512]{1,0:T(8,128)S(1)} custom-call(s32[2]{0:T(128)} %lengths.3, s32[28]{0:T(128)} %hid_kind.3, s32[28]{0:T(128)} %hid_sign.3, s32[8]{0:T(128)} %out_kind.3, s32[8]{0:T(128)} %out_sign.3, bf16[8,32,128]{2,1,0:T(8,128)(2,1)} %bitcast.2, bf16[8,32,128]{2,1,0:T(8,128)(2,1)} %bitcast.4, bf16[1024,3584]{1,0:T(8,128)(2,1)} %hidden.3, ...), custom_call_target="tpu_custom_call" | custom-call | tf_op jit(solution)/shard_map/sketch_away/pallas_call | solution.py:82
  3.7 2.6 %collective-permute-start = (f32[64,512]{1,0:T(8,128)S(1)}, f32[64,512]{1,0:T(8,128)S(1)}, u32[]{:S(2)}, u32[]{:S(2)}) collective-permute-start(f32[64,512]{1,0:T(8,128)S(1)} %sketch_away.1), channel_id=1, source_target_pairs={{0,1},{1,0},{2,3},{3,2},{4,5},{5,4},{6,7},{7,6},{8,9},{9,8},{10,11... | collective-permute-start | bytes 393224 | tf_op jit(solution)/shard_map/ppermute | solution.py:296
  6.2 3.7 %sketch_own.1 = f32[64,512]{1,0:T(8,128)S(1)} custom-call(s32[2]{0:T(128)} %lengths.3, s32[28]{0:T(128)} %hid_kind.3, s32[28]{0:T(128)} %hid_sign.3, s32[8]{0:T(128)} %out_kind.3, s32[8]{0:T(128)} %out_sign.3, bf16[8,32,128]{2,1,0:T(8,128)(2,1)} %bitcast.3, bf16[8,32,128]{2,1,0:T(8,128)(2,1)} %bitcast.5, bf16[1024,3584]{1,0:T(8,128)(2,1)} %hidden.3, ...), custom_call_target="tpu_custom_call" | custom-call | tf_op jit(solution)/shard_map/sketch_own/pallas_call | solution.py:82
  9.9 0.0 collective-permute-done
  10.0 4.8 %collective-permute-start.1 = (f32[64,512]{1,0:T(8,128)S(1)}, f32[64,512]{1,0:T(8,128)S(1)}, u32[]{:S(2)}, u32[]{:S(2)}) collective-permute-start(f32[64,512]{1,0:T(8,128)S(1)} %add.6), channel_id=1, source_target_pairs={{0,7},{1,2},{2,1},{3,4},{4,3},{5,6},{6,5},{7,0},{8,15},{9,10},{10,... | collective-permute-start | bytes 393224 | tf_op jit(solution)/shard_map/ppermute | solution.py:296
  14.7 2.4 %collective-permute-done.1 = f32[64,512]{1,0:T(8,128)S(1)} collective-permute-done((f32[64,512]{1,0:T(8,128)S(1)}, f32[64,512]{1,0:T(8,128)S(1)}, u32[]{:S(2)}, u32[]{:S(2)}) %collective-permute-start.1) | collective-permute-done | bytes 131104 | tf_op jit(solution)/shard_map/ppermute | solution.py:296
  17.1 1.7 %collective-permute-start.2 = (f32[64,512]{1,0:T(8,128)S(1)}, f32[64,512]{1,0:T(8,128)S(1)}, u32[]{:S(2)}, u32[]{:S(2)}) collective-permute-start(f32[64,512]{1,0:T(8,128)S(1)} %add.7.x_ref), channel_id=1, source_target_pairs={{0,3},{1,6},{2,5},{3,0},{4,7},{5,2},{6,1},{7,4},{8,11},{9,14},{10,... | collective-permute-start | bytes 393224 | tf_op jit(solution)/shard_map/ppermute | solution.py:296
  18.8 5.4 %collective-permute-done.2.other = f32[64,512]{1,0:T(8,128)S(1)} collective-permute-done((f32[64,512]{1,0:T(8,128)S(1)}, f32[64,512]{1,0:T(8,128)S(1)}, u32[]{:S(2)}, u32[]{:S(2)}) %collective-permute-start.2) | collective-permute-done | bytes 131104 | tf_op jit(solution)/shard_map/ppermute | solution.py:296
  24.2 1.0 %outer.1 = f32[64,8,128]{2,1,0:T(8,128)} custom-call(f32[64,512]{1,0:T(8,128)S(1)} %add.7.x_ref, f32[64,512]{1,0:T(8,128)S(1)} %collective-permute-done.2.other), custom_call_target="tpu_custom_call" | custom-call | tf_op jit(solution)/shard_map/outer/pallas_call | solution.py:136
  25.2 10.5 %all-to-all-start = ((f32[64,8,128]{2,1,0:T(8,128)}), f32[64,8,128]{2,1,0:T(8,128)S(1)}, u32[]{:S(2)}, u32[]{:S(2)}) async-start(f32[64,8,128]{2,1,0:T(8,128)} %outer.1), calls=%async_computation | async-start | bytes 524288 | tf_op jit(solution)/shard_map/all_to_all | solution.py:303
  36.4 9.0 %all-to-all-done.gathered = f32[64,8,128]{2,1,0:T(8,128)S(1)} async-done(((f32[64,8,128]{2,1,0:T(8,128)}), f32[64,8,128]{2,1,0:T(8,128)S(1)}, u32[]{:S(2)}, u32[]{:S(2)}) %all-to-all-start) | async-done | bytes 262176 | tf_op jit(solution)/shard_map/all_to_all | solution.py:303
  45.4 4.5 %whiten.1 = f32[2,1024]{1,0:T(2,128)} custom-call(f32[1]{0:T(128)S(6)} %copy.11.ridge, f32[64,8,128]{2,1,0:T(8,128)S(1)} %all-to-all-done.gathered), custom_call_target="tpu_custom_call" | custom-call | tf_op jit(solution)/shard_map/whiten/pallas_call | solution.py:266
  (2 shorter events, 0.0 us)
Async XLA Ops:
  3.7 6.3 %collective-permute-start = (f32[64,512]{1,0:T(8,128)S(1)}, f32[64,512]{1,0:T(8,128)S(1)}, u32[]{:S(2)}, u32[]{:S(2)}) collective-permute-start(f32[64,512]{1,0:T(8,128)S(1)} %sketch_away.1), channel_id=1, source_target_pairs={{0,1},{1,0},{2,3},{3,2},{4,5},{5,4},{6,7},{7,6},{8,9},{9,8},{10,11... | collective-permute-start | bytes 393224 | tf_op jit(solution)/shard_map/ppermute | solution.py:296
  10.0 7.1 %collective-permute-start.1 = (f32[64,512]{1,0:T(8,128)S(1)}, f32[64,512]{1,0:T(8,128)S(1)}, u32[]{:S(2)}, u32[]{:S(2)}) collective-permute-start(f32[64,512]{1,0:T(8,128)S(1)} %add.6), channel_id=1, source_target_pairs={{0,7},{1,2},{2,1},{3,4},{4,3},{5,6},{6,5},{7,0},{8,15},{9,10},{10,... | collective-permute-start | bytes 393224 | tf_op jit(solution)/shard_map/ppermute | solution.py:296
  17.1 7.1 %collective-permute-start.2 = (f32[64,512]{1,0:T(8,128)S(1)}, f32[64,512]{1,0:T(8,128)S(1)}, u32[]{:S(2)}, u32[]{:S(2)}) collective-permute-start(f32[64,512]{1,0:T(8,128)S(1)} %add.7.x_ref), channel_id=1, source_target_pairs={{0,3},{1,6},{2,5},{3,0},{4,7},{5,2},{6,1},{7,4},{8,11},{9,14},{10,... | collective-permute-start | bytes 393224 | tf_op jit(solution)/shard_map/ppermute | solution.py:296
  25.2 20.2 %all-to-all-start = ((f32[64,8,128]{2,1,0:T(8,128)}), f32[64,8,128]{2,1,0:T(8,128)S(1)}, u32[]{:S(2)}, u32[]{:S(2)}) async-start(f32[64,8,128]{2,1,0:T(8,128)} %outer.1), calls=%async_computation | async-start | bytes 524288 | tf_op jit(solution)/shard_map/all_to_all | solution.py:303
